TPU v7x, 32 devices: a whole 2x2x4 slice. The times are simulated.
32 devices in a mesh: dp: 4 (over x, core), blk: 8 (over z, y).
Axes of the slice: x: 2, y: 2, z: 4, core: 2. Of those that a mesh axis runs over, the one named last changes fastest.
Arguments:
- frames: bfloat16 [4, 1024, 768], P('dp', 'blk'), may hold values from -6 to 6
- segment: int32 [4, 1024], P('dp', 'blk'), may hold values from -1 to 16, as said below
- conv_weight: bfloat16 [768, 48, 128], replicated, may hold values from -0.078125 to 0.078125
- conv_bias: bfloat16 [768], replicated, may hold values from -1.5 to 1.5
- qkv_weight: bfloat16 [768, 2304], replicated, may hold values from -0.21875 to 0.21875
- qv_bias: bfloat16 [1536], replicated, may hold values from -1.5 to 1.5
- out_weight: bfloat16 [768, 768], replicated, may hold values from -0.875 to 0.875
- out_bias: bfloat16 [768], replicated, may hold values from -1.5 to 1.5
- norm1_gain: bfloat16 [768], replicated, may hold values from 0.25 to 1.75
- norm1_bias: bfloat16 [768], replicated, may hold values from -1.5 to 1.5
- ffn_in: bfloat16 [768, 3072], replicated, may hold values from -0.21875 to 0.21875
- ffn_in_bias: bfloat16 [3072], replicated, may hold values from -1.5 to 1.5
- ffn_out: bfloat16 [3072, 768], replicated, may hold values from -0.109375 to 0.109375
- ffn_out_bias: bfloat16 [768], replicated, may hold values from -1.5 to 1.5
- norm2_gain: bfloat16 [768], replicated, may hold values from 0.25 to 1.75
- norm2_bias: bfloat16 [768], replicated, may hold values from -1.5 to 1.5
- cotangent: bfloat16 [4, 1024, 768], P('dp', 'blk'), may hold values from -6 to 6
Outputs:
- layer_out: bfloat16 [4, 1024, 768], P('dp', 'blk')
- frames_grad: bfloat16 [4, 1024, 768], P('dp', 'blk')
- conv_weight_grad: float32 [768, 48, 128], P('blk')
- conv_bias_grad: float32 [768], P('blk')
- qkv_weight_grad: float32 [768, 2304], P('blk')
- qv_bias_grad: float32 [1536], P('blk')
- out_weight_grad: float32 [768, 768], P('blk')
- out_bias_grad: float32 [768], P('blk')
- norm1_gain_grad: float32 [768], P('blk')
- norm1_bias_grad: float32 [768], P('blk')
- ffn_in_grad: float32 [768, 3072], P('blk')
- ffn_in_bias_grad: float32 [3072], P('blk')
- ffn_out_grad: float32 [3072, 768], P('blk')
- ffn_out_bias_grad: float32 [768], P('blk')
- norm2_gain_grad: float32 [768], P('blk')
- norm2_bias_grad: float32 [768], P('blk')
Inputs may be any that keep to these rules, and one draw needn't show every extreme that they name: `segment`: in each row the frames of a clip are consecutive and clips are numbered 0, 1, 2, ... in order; padding frames, if any, close the row. At least one row holds a clip that starts in the row's first 128 frames and ends in its last 128.
All inputs are finite; a program needn't handle non-finite values.
Results may differ from a plain program's by a relative error of at most 0.02.
Values may be sent and summed in bfloat16 or wider, within the bound.
A program may use at most 320 MiB of HBM per device.

v0:
```python
import functools
import math
import types

import jax
import jax.numpy as jnp
from jax import lax
from jax.experimental import pallas as pl
from jax.experimental.pallas import tpu as pltpu
from jax.sharding import PartitionSpec as P

HEADS = 12
GROUPS = 16


EPS = 1e-05
ROOT_HALF = 0.7071067811865476
DENSITY_CONST = 0.3989422804014327


def with_halo(x, sides, width):
    for axis, dim in sides:
        size, length = (lax.axis_size(axis), x.shape[dim])
        up = [(i, (i + 1) % size) for i in range(size - 1)]
        down = [(j, i) for i, j in up]
        last = lax.slice_in_dim(x, length - width, length, axis=dim)
        initial = lax.slice_in_dim(x, 0, width, axis=dim)
        before = lax.ppermute(last, axis, up)
        after = lax.ppermute(initial, axis, down)
        x = jnp.concatenate([before, x, after], axis=dim)
    return x


def from_behind(value, axis, steps):
    count = lax.axis_size(axis)
    pairs = [(source, (source + steps) % count) for source in range(count)]
    return lax.ppermute(value, axis, pairs)


def gelu_value(signal):
    return 0.5 * signal * (1.0 + lax.erf(signal * ROOT_HALF))


def gelu_slope(signal):
    return (
        0.5 * (1.0 + lax.erf(signal * ROOT_HALF))
        + signal * jnp.exp(-0.5 * signal * signal) * DENSITY_CONST
    )


def norm_forward(signal, gain_vec, shift_vec):
    average = jnp.mean(signal, axis=-1, keepdims=True)
    centred = signal - average
    inv_std = lax.rsqrt(jnp.mean(centred * centred, axis=-1, keepdims=True) + EPS)
    normed = centred * inv_std
    return (normed * gain_vec + shift_vec, normed, inv_std)


def norm_backward(grad_in, normed, inv_std, gain_vec):
    scaled = grad_in * gain_vec
    result = inv_std * (
        scaled
        - jnp.mean(scaled, axis=-1, keepdims=True)
        - normed * jnp.mean(scaled * normed, axis=-1, keepdims=True)
    )
    return (result, jnp.sum(grad_in * normed, axis=0), jnp.sum(grad_in, axis=0))


def block_grads(
    query_h, dout_h, query_seg, log_tot, row_delta, key_h, value_h, key_seg, score_scale
):
    scores = (
        jnp.einsum("rqhc,rkhc->rhqk", query_h, key_h, preferred_element_type=jnp.float32)
        * score_scale
    )
    same_seg = (query_seg[:, :, None] == key_seg[:, None, :])[:, None]
    weights_f = jnp.where(same_seg, jnp.exp(scores - log_tot[..., None]), 0.0)
    grad_prob = jnp.einsum("rqhc,rkhc->rhqk", dout_h, value_h, preferred_element_type=jnp.float32)
    grad_score = (weights_f * (grad_prob - row_delta[..., None])).astype(jnp.bfloat16)
    query_part = score_scale * jnp.einsum(
        "rhqk,rkhc->rqhc", grad_score, key_h, preferred_element_type=jnp.float32
    )
    key_part = score_scale * jnp.einsum(
        "rhqk,rqhc->rkhc", grad_score, query_h, preferred_element_type=jnp.float32
    )
    value_part = jnp.einsum(
        "rhqk,rqhc->rkhc",
        weights_f.astype(jnp.bfloat16),
        dout_h,
        preferred_element_type=jnp.float32,
    )
    return (query_part, key_part, value_part)


def ring_shards(
    frames,
    segment,
    conv_weight,
    conv_bias,
    qkv_weight,
    qv_bias,
    out_weight,
    out_bias,
    norm1_gain,
    norm1_bias,
    ffn_in,
    ffn_in_bias,
    ffn_out,
    ffn_out_bias,
    norm2_gain,
    norm2_bias,
    cotangent,
):
    row_count, block_len, model_width = frames.shape
    token_count = row_count * block_len
    group_width = conv_weight.shape[1]
    kernel = conv_weight.shape[2]
    half_kernel = kernel // 2
    head_dim = model_width // HEADS
    score_scale = head_dim ** (-0.5)
    cycle_len = lax.axis_size("blk")
    is_valid = segment >= 0
    masked = jnp.where(is_valid[..., None], frames, jnp.zeros_like(frames))
    padded = with_halo(masked, (("blk", 1),), half_kernel)
    conv_out = lax.conv_general_dilated(
        padded,
        conv_weight,
        (1,),
        "VALID",
        dimension_numbers=("NWC", "OIW", "NWC"),
        feature_group_count=GROUPS,
        preferred_element_type=jnp.float32,
    )
    pre_conv = conv_out[:, :block_len].reshape(token_count, model_width) + conv_bias.astype(
        jnp.float32
    )
    mixed_in = frames.reshape(token_count, model_width).astype(jnp.float32) + gelu_value(pre_conv)
    mixed_low = mixed_in.astype(jnp.bfloat16)
    pair_bias = qv_bias.astype(jnp.float32)
    zero_bias = jnp.zeros((model_width,), jnp.float32)
    full_bias = jnp.concatenate([pair_bias[:model_width], zero_bias, pair_bias[model_width:]])
    project = (
        jnp.dot(mixed_low, qkv_weight, preferred_element_type=jnp.float32) + full_bias
    ).astype(jnp.bfloat16)
    project = project.reshape(row_count, block_len, 3 * model_width)
    query_heads = project[..., :model_width].reshape(row_count, block_len, HEADS, head_dim)
    keys_local = project[..., model_width : 2 * model_width]
    values_local = project[..., 2 * model_width :]
    key_heads = keys_local.reshape(row_count, block_len, HEADS, head_dim)
    value_heads = values_local.reshape(row_count, block_len, HEADS, head_dim)
    query_seg = segment.astype(jnp.bfloat16)
    start_carry = (
        jnp.full((row_count, HEADS, block_len), -1e30, jnp.float32),
        jnp.zeros((row_count, HEADS, block_len), jnp.float32),
        jnp.zeros((row_count, HEADS, block_len, head_dim), jnp.float32),
    )
    key_piece = lax.all_gather(keys_local, "blk", axis=1, tiled=True)
    value_piece = lax.all_gather(values_local, "blk", axis=1, tiled=True)
    seg_piece = lax.all_gather(query_seg, "blk", axis=1, tiled=True)
    piece_len = key_piece.shape[1]
    block_size = math.gcd(piece_len, 512)

    def one_block(block_index, inner_carry):
        running_max, denominator, numerator = inner_carry
        offset = block_index * block_size
        key_block = lax.dynamic_slice_in_dim(key_piece, offset, block_size, 1).reshape(
            row_count, block_size, HEADS, head_dim
        )
        value_block = lax.dynamic_slice_in_dim(value_piece, offset, block_size, 1).reshape(
            row_count, block_size, HEADS, head_dim
        )
        seg_block = lax.dynamic_slice_in_dim(seg_piece, offset, block_size, 1)
        scores = (
            jnp.einsum(
                "rqhc,rkhc->rhqk", query_heads, key_block, preferred_element_type=jnp.float32
            )
            * score_scale
        )
        same_seg = (query_seg[:, :, None] == seg_block[:, None, :])[:, None]
        masked_scores = jnp.where(same_seg, scores, -1e30)
        new_max = jnp.maximum(running_max, jnp.max(masked_scores, axis=-1))
        weights_f = jnp.where(same_seg, jnp.exp(masked_scores - new_max[..., None]), 0.0)
        rescale = jnp.exp(running_max - new_max)
        denominator = denominator * rescale + jnp.sum(weights_f, axis=-1)
        numerator = numerator * rescale[..., None] + jnp.einsum(
            "rhqk,rkhc->rhqc",
            weights_f.astype(jnp.bfloat16),
            value_block,
            preferred_element_type=jnp.float32,
        )
        return (new_max, denominator, numerator)

    running_max, denominator, numerator = lax.fori_loop(
        0, piece_len // block_size, one_block, start_carry
    )
    log_total = running_max + jnp.log(denominator)
    attended_heads = (numerator / denominator[..., None]).transpose(0, 2, 1, 3)
    attended = attended_heads.reshape(token_count, model_width)
    attn_low = attended.astype(jnp.bfloat16)
    branch = jnp.dot(attn_low, out_weight, preferred_element_type=jnp.float32) + out_bias.astype(
        jnp.float32
    )
    gain_one = norm1_gain.astype(jnp.float32)
    hidden_norm, normed_one, inv_one = norm_forward(
        mixed_in + branch, gain_one, norm1_bias.astype(jnp.float32)
    )
    hidden_low = hidden_norm.astype(jnp.bfloat16)
    ffn_pre = jnp.dot(hidden_low, ffn_in, preferred_element_type=jnp.float32) + ffn_in_bias.astype(
        jnp.float32
    )
    ffn_act = gelu_value(ffn_pre).astype(jnp.bfloat16)
    ffn_branch = jnp.dot(
        ffn_act, ffn_out, preferred_element_type=jnp.float32
    ) + ffn_out_bias.astype(jnp.float32)
    gain_two = norm2_gain.astype(jnp.float32)
    layer_out, normed_two, inv_two = norm_forward(
        hidden_norm + ffn_branch, gain_two, norm2_bias.astype(jnp.float32)
    )
    grad_top = cotangent.reshape(token_count, model_width).astype(jnp.float32)
    grad_second, norm2_gain_grad, norm2_bias_grad = norm_backward(
        grad_top, normed_two, inv_two, gain_two
    )
    grad_branch_two = grad_second.astype(jnp.bfloat16)
    ffn_out_grad = jnp.einsum(
        "nf,nd->fd", ffn_act, grad_branch_two, preferred_element_type=jnp.float32
    )
    ffn_out_bias_grad = jnp.sum(grad_branch_two.astype(jnp.float32), axis=0)
    grad_act = jnp.einsum("nd,fd->nf", grad_branch_two, ffn_out, preferred_element_type=jnp.float32)
    grad_pre = (grad_act * gelu_slope(ffn_pre)).astype(jnp.bfloat16)
    ffn_in_grad = jnp.einsum("nd,nf->df", hidden_low, grad_pre, preferred_element_type=jnp.float32)
    ffn_in_bias_grad = jnp.sum(grad_pre.astype(jnp.float32), axis=0)
    grad_hidden = grad_second + jnp.einsum(
        "nf,df->nd", grad_pre, ffn_in, preferred_element_type=jnp.float32
    )
    grad_first, norm1_gain_grad, norm1_bias_grad = norm_backward(
        grad_hidden, normed_one, inv_one, gain_one
    )
    grad_branch = grad_first.astype(jnp.bfloat16)
    out_weight_grad = jnp.einsum(
        "ne,nd->ed", attn_low, grad_branch, preferred_element_type=jnp.float32
    )
    out_bias_grad = jnp.sum(grad_branch.astype(jnp.float32), axis=0)
    grad_att = jnp.einsum("nd,ed->ne", grad_branch, out_weight, preferred_element_type=jnp.float32)
    grad_heads = grad_att.astype(jnp.bfloat16).reshape(row_count, block_len, HEADS, head_dim)
    row_delta = jnp.einsum("rqhc,rqhc->rhq", grad_heads.astype(jnp.float32), attended_heads)
    zero_heads = jnp.zeros((row_count, block_len, HEADS, head_dim), jnp.float32)

    def key_step(carried):
        key_block, value_block, seg_block, key_grad, value_grad, query_grad = carried
        query_part, key_part, value_part = block_grads(
            query_heads,
            grad_heads,
            query_seg,
            log_total,
            row_delta,
            key_block,
            value_block,
            seg_block,
            score_scale,
        )
        query_grad = query_grad + query_part
        key_grad = key_grad + key_part
        value_grad = value_grad + value_part
        key_block, value_block, seg_block = from_behind(
            (key_block, value_block, seg_block), "blk", 1
        )
        key_grad, value_grad = (
            from_behind(key_grad.astype(jnp.bfloat16), "blk", 1).astype(key_grad.dtype),
            from_behind(value_grad.astype(jnp.bfloat16), "blk", 1).astype(value_grad.dtype),
        )
        return (key_block, value_block, seg_block, key_grad, value_grad, query_grad)

    def four_steps(turn_index, carried):
        for repeat in range(4):
            carried = key_step(carried)
        return carried

    final_state = lax.fori_loop(
        0,
        cycle_len // 4,
        four_steps,
        (key_heads, value_heads, query_seg, zero_heads, zero_heads, zero_heads),
    )
    key_grad, value_grad, query_grad = (final_state[3], final_state[4], final_state[5])
    grad_project = jnp.concatenate(
        [
            query_grad.reshape(token_count, model_width),
            key_grad.reshape(token_count, model_width),
            value_grad.reshape(token_count, model_width),
        ],
        axis=1,
    ).astype(jnp.bfloat16)
    qkv_weight_grad = jnp.einsum(
        "nd,ne->de", mixed_low, grad_project, preferred_element_type=jnp.float32
    )
    bias_sums = jnp.sum(grad_project.astype(jnp.float32), axis=0)
    qv_bias_grad = jnp.concatenate([bias_sums[:model_width], bias_sums[2 * model_width :]])
    grad_mixed = grad_first + jnp.einsum(
        "ne,de->nd", grad_project, qkv_weight, preferred_element_type=jnp.float32
    )
    grad_conv = (grad_mixed * gelu_slope(pre_conv)).astype(jnp.bfloat16)
    conv_bias_grad = jnp.sum(grad_conv.astype(jnp.float32), axis=0)
    grad_conv_rows = grad_conv.reshape(row_count, block_len, model_width)
    grad_padded = with_halo(grad_conv_rows, (("blk", 1),), half_kernel)
    flipped = conv_weight.reshape(GROUPS, group_width, group_width, kernel).transpose(0, 2, 1, 3)
    flipped = flipped.reshape(model_width, group_width, kernel)[:, :, ::-1]
    back_conv = lax.conv_general_dilated(
        grad_padded,
        flipped,
        (1,),
        "VALID",
        dimension_numbers=("NWC", "OIW", "NWC"),
        feature_group_count=GROUPS,
        preferred_element_type=jnp.float32,
    )[:, 1:]
    frames_grad = (
        grad_mixed.reshape(row_count, block_len, model_width)
        + jnp.where(is_valid[..., None], back_conv, 0.0)
    ).astype(jnp.bfloat16)
    conv_weight_grad = lax.conv_general_dilated(
        padded,
        grad_conv_rows,
        (1,),
        "VALID",
        dimension_numbers=("CWN", "IWO", "CNW"),
        batch_group_count=GROUPS,
        preferred_element_type=jnp.float32,
    )[:, :, :kernel]
    (
        conv_weight_part,
        conv_bias_part,
        qkv_weight_part,
        qv_bias_part,
        out_weight_part,
        out_bias_part,
        gain_one_part,
        shift_one_part,
        ffn_in_part,
        ffn_in_bias_part,
        ffn_out_part,
        ffn_out_bias_part,
        gain_two_part,
        shift_two_part,
    ) = (
        lax.psum_scatter(conv_weight_grad, "blk", scatter_dimension=0, tiled=True),
        lax.psum_scatter(conv_bias_grad, "blk", scatter_dimension=0, tiled=True),
        lax.psum_scatter(qkv_weight_grad, "blk", scatter_dimension=0, tiled=True),
        lax.psum_scatter(qv_bias_grad, "blk", scatter_dimension=0, tiled=True),
        lax.psum_scatter(out_weight_grad, "blk", scatter_dimension=0, tiled=True),
        lax.psum_scatter(out_bias_grad, "blk", scatter_dimension=0, tiled=True),
        lax.psum_scatter(norm1_gain_grad, "blk", scatter_dimension=0, tiled=True),
        lax.psum_scatter(norm1_bias_grad, "blk", scatter_dimension=0, tiled=True),
        lax.psum_scatter(ffn_in_grad, "blk", scatter_dimension=0, tiled=True),
        lax.psum_scatter(ffn_in_bias_grad, "blk", scatter_dimension=0, tiled=True),
        lax.psum_scatter(ffn_out_grad, "blk", scatter_dimension=0, tiled=True),
        lax.psum_scatter(ffn_out_bias_grad, "blk", scatter_dimension=0, tiled=True),
        lax.psum_scatter(norm2_gain_grad, "blk", scatter_dimension=0, tiled=True),
        lax.psum_scatter(norm2_bias_grad, "blk", scatter_dimension=0, tiled=True),
    )
    totals = (
        lax.psum(conv_weight_part.astype(jnp.bfloat16), "dp").astype(jnp.float32),
        lax.psum(conv_bias_part.astype(jnp.bfloat16), "dp").astype(jnp.float32),
        lax.psum(qkv_weight_part.astype(jnp.bfloat16), "dp").astype(jnp.float32),
        lax.psum(qv_bias_part.astype(jnp.bfloat16), "dp").astype(jnp.float32),
        lax.psum(out_weight_part.astype(jnp.bfloat16), "dp").astype(jnp.float32),
        lax.psum(out_bias_part.astype(jnp.bfloat16), "dp").astype(jnp.float32),
        lax.psum(gain_one_part.astype(jnp.bfloat16), "dp").astype(jnp.float32),
        lax.psum(shift_one_part.astype(jnp.bfloat16), "dp").astype(jnp.float32),
        lax.psum(ffn_in_part.astype(jnp.bfloat16), "dp").astype(jnp.float32),
        lax.psum(ffn_in_bias_part.astype(jnp.bfloat16), "dp").astype(jnp.float32),
        lax.psum(ffn_out_part.astype(jnp.bfloat16), "dp").astype(jnp.float32),
        lax.psum(ffn_out_bias_part.astype(jnp.bfloat16), "dp").astype(jnp.float32),
        lax.psum(gain_two_part.astype(jnp.bfloat16), "dp").astype(jnp.float32),
        lax.psum(shift_two_part.astype(jnp.bfloat16), "dp").astype(jnp.float32),
    )
    return (
        layer_out.reshape(row_count, block_len, model_width).astype(jnp.bfloat16),
        frames_grad,
        totals[0],
        totals[1],
        totals[2],
        totals[3],
        totals[4],
        totals[5],
        totals[6],
        totals[7],
        totals[8],
        totals[9],
        totals[10],
        totals[11],
        totals[12],
        totals[13],
    )


MESH = pl.DeviceIdType.MESH
LANES = 128
TAP_STEP = 16
VMEM = pl.BlockSpec(memory_space=pltpu.VMEM)


def peer(me, step, count):
    return lax.rem(me + step, count)


def greet(index, count, rows):
    barrier = pltpu.get_barrier_semaphore()
    for step in range(1, count * rows):
        other = lax.rem(index + step, count * rows)
        pl.semaphore_signal(
            barrier,
            inc=1,
            device_id={"dp": other // count, "blk": lax.rem(other, count)},
            device_id_type=MESH,
        )


def greet_wait(count, rows):
    pl.semaphore_wait(pltpu.get_barrier_semaphore(), count * rows - 1)


def remote(src, dst, send_sem, recv_sem, target, axis="blk"):
    copy = pltpu.make_async_remote_copy(
        src_ref=src,
        dst_ref=dst,
        send_sem=send_sem,
        recv_sem=recv_sem,
        device_id=target if isinstance(target, dict) else {axis: target},
        device_id_type=MESH,
    )
    copy.start()
    return copy


def turned(value):
    return value.astype(jnp.float32).T.astype(jnp.bfloat16)


def matmul_turned(left, right):
    return lax.dot_general(
        left, right, (((1,), (1,)), ((), ())), preferred_element_type=jnp.float32
    )


def sum_parts(parts_ref):
    total = parts_ref[0].astype(jnp.float32)
    for part in range(1, parts_ref.shape[0]):
        total = total + parts_ref[part].astype(jnp.float32)
    return total


def lane_block(index):
    return pl.ds(pl.multiple_of(index * LANES, LANES), LANES)


def row_block(index, size):
    return pl.ds(pl.multiple_of(index * size, size), size)


def swap_blocks(tiles, width):
    count = len(tiles)
    lane = lax.broadcasted_iota(jnp.int32, tiles[0].shape, 1) // width
    tiles = list(tiles)
    step = count // 2
    while step:
        low = (lane & step) == 0
        for u in range(count):
            if u & step == 0:
                one, two = tiles[u], tiles[u + step]
                tiles[u] = jnp.where(low, one, pltpu.roll(two, step * width, 1))
                tiles[u + step] = jnp.where(low, pltpu.roll(one, LANES - step * width, 1), two)
        step //= 2
    return tiles


def spread_taps(source, offset, direction, stage_ref, out_ref):
    rows, length = source.shape
    blocks = out_ref.shape[1] // LANES
    for tap in range(TAP_STEP):
        shift = (length - offset - direction * tap) % length
        moved = pltpu.roll(source, shift, 1)
        for block in range(blocks):
            first = block * rows * TAP_STEP + tap
            stage_ref[pl.ds(first, rows, stride=TAP_STEP), :] = moved[
                :, block * LANES : (block + 1) * LANES
            ]
    size = rows * TAP_STEP
    for block in range(blocks):
        out_ref[:, block * LANES : (block + 1) * LANES] = stage_ref[
            block * size : (block + 1) * size, :
        ].astype(jnp.bfloat16)


def query_span(index, size):
    return pl.ds(pl.multiple_of(index * size, size), size)


def same_clip(column_ref, seg_row):
    column = column_ref[...]
    parts = [
        column == seg_row[:, start : start + LANES]
        for start in range(0, seg_row.shape[1], LANES)
    ]
    return jnp.concatenate(parts, axis=1)


def clip_column(count, segs_ref, column_ref):
    for block in range(count):
        row = segs_ref[block].astype(jnp.float32)
        column_ref[block * LANES : (block + 1) * LANES, :] = jnp.broadcast_to(
            row, (LANES, LANES)
        ).T


def clip_row(segs_ref, first, size):
    parts = [segs_ref[first + i].astype(jnp.float32) for i in range(size // LANES)]
    return jnp.concatenate(parts, axis=1)


def layer_kernel(names, count, rows_count, head_dim, *refs):
    R = types.SimpleNamespace(**dict(zip(names, refs)))
    low, f32 = jnp.bfloat16, jnp.float32
    me, row = lax.axis_index("blk"), lax.axis_index("dp")
    level, side = me // 2, lax.rem(me, 2)
    levels = count // 2
    half = count // 2
    near = me + 1 - 2 * side
    core = lax.rem(row, 2)
    twin = row + 1 - 2 * core
    upper = level // 2
    pos = 4 * core + 2 * lax.rem(level, 2) + side
    home_row = 2 * (row // 2) + upper
    at_home = core == upper
    across = peer(row, 2, rows_count)
    tokens, width = R.frames.shape
    channels = width // count
    length = count * LANES
    group_width = R.own_weight.shape[1]
    groups = channels // group_width
    steps = LANES // TAP_STEP
    scale = head_dim ** (-0.5)
    chunks = R.in_hbm.shape[1] // width

    def send(kind, step, source, target_ref, target, axis="blk"):
        return remote(
            source, target_ref, R.out_sem.at[kind, step], R.in_sem.at[kind, step], target, axis
        )

    def wait(copies):
        for copy in copies:
            copy.wait()

    def to_blocks(kind, source, target_ref):
        copies = []
        for step in range(1, count):
            target = peer(me, step, count)
            copies.append(send(kind, step, source(target), target_ref, target))
        return copies

    def device_at(place, part):
        return {"dp": 2 * (row // 2) + place // 4, "blk": 4 * part + lax.rem(place, 4)}

    def to_places(kind, source, target_ref):
        copies = []
        for step in range(1, count):
            target = peer(pos, step, count)
            copies.append(send(kind, step, source(target), target_ref, device_at(target, upper)))
        return copies

    def move(kind, source, target_ref, device):
        copy = pltpu.make_async_remote_copy(
            src_ref=source,
            dst_ref=target_ref,
            send_sem=R.out_sem.at[kind, 0],
            recv_sem=R.in_sem.at[kind, 0],
            device_id=device,
            device_id_type=MESH,
        )
        away = jnp.logical_not(at_home)
        pl.when(away)(copy.start)

        @pl.when(at_home)
        def _():
            target_ref[...] = source[...]

        return [(away, away, copy)]

    def shift_all(kind, first, own, device_of, source, target_ref):
        pending = []
        for step in range(count):
            target = peer(first, step, count)
            away = jnp.logical_not(jnp.logical_and(at_home, target == own))
            copy = pltpu.make_async_remote_copy(
                src_ref=source(target),
                dst_ref=target_ref,
                send_sem=R.out_sem.at[kind, step],
                recv_sem=R.in_sem.at[kind, step],
                device_id=device_of(target),
                device_id_type=MESH,
            )
            pl.when(away)(copy.start)
            pending.append((away, away, copy))

        @pl.when(at_home)
        def _():
            target_ref[...] = source(own)[...]

        return pending

    def to_level(kind, source, target_ref):
        return shift_all(
            kind, me, pos, lambda place: device_at(place, core), source, target_ref
        )

    def from_level(kind, source, target_ref):
        return shift_all(
            kind, pos, me, lambda block: {"dp": home_row, "blk": block}, source, target_ref
        )

    def wait_some(pending):
        for sends, comes, copy in pending:
            pl.when(sends)(copy.wait_send)
            pl.when(comes)(copy.wait_recv)

    def chunk_of(index):
        return slice(index * width, (index + 1) * width)

    def table(index):
        return R.table[index : index + 1, :]

    def dot(left, right):
        return jnp.dot(left, right, preferred_element_type=f32)

    greet(row * count + me, count, rows_count)

    loads = [pltpu.make_async_copy(R.qkv_hbm, R.qkv_w, R.load_sem.at[0])]
    loads.append(pltpu.make_async_copy(R.out_hbm, R.out_w, R.load_sem.at[1]))
    for chunk in range(chunks):
        span = chunk_of(chunk)
        loads.append(
            pltpu.make_async_copy(
                R.in_hbm.at[:, span], R.in_w.at[:, span], R.load_sem.at[2 + 2 * chunk]
            )
        )
        loads.append(
            pltpu.make_async_copy(
                R.back_hbm.at[span], R.back_w.at[span], R.load_sem.at[3 + 2 * chunk]
            )
        )
    for load in loads:
        load.start()
    own_load = pltpu.make_async_copy(
        R.conv_hbm.at[row_block(me, channels)], R.own_weight, R.load_sem.at[2 + 2 * chunks]
    )
    own_load.start()
    valid = (R.segment[...] >= 0).astype(f32)
    R.turned[...] = (R.frames[...].astype(f32).T * valid).astype(low)
    to_level_device = device_at(me, core)
    from_level_device = {"dp": home_row, "blk": pos}

    R.table[...] = jnp.zeros_like(R.table)
    R.small[...] = jnp.zeros_like(R.small)
    place = 0
    for vector in VECTORS:
        ref = getattr(R, vector)
        for part in range(ref.shape[0] // width):
            R.table[place, :] = ref[chunk_of(part)].astype(f32)
            place += 1

    def mix_taps(mix, tile_rows):
        @pl.loop(0, group_width // steps)
        def _(block):
            for group in range(groups):
                tiles = [
                    R.stage[tile_rows(group, block * steps + u), :] for u in range(steps)
                ]
                for a, tile in enumerate(swap_blocks(tiles, TAP_STEP)):
                    rows = slice(a * group_width, (a + 1) * group_width)
                    mix[group, rows, lane_block(block)] = tile.astype(low)

    square = group_width * group_width
    own_load.wait()
    total_rows = channels * group_width
    R.stage[:total_rows, :] = R.own_weight[...].astype(f32).reshape(total_rows, LANES)
    mix_taps(R.mix, lambda g, i: pl.ds(g * square + i, group_width, stride=group_width))
    greet_wait(count, rows_count)

    copies = to_blocks(
        0, lambda p: R.turned.at[row_block(p, channels), :], R.column.at[:, lane_block(me + 1)]
    )
    brought = move(33, R.frames, R.frames_home, to_level_device)
    seg_pending = to_level(1, lambda p: R.segment, R.segs.at[me])
    R.column[:, lane_block(me + 1)] = R.turned[row_block(me, channels), :]
    for ref in (R.column, R.gcol):
        ref[:, :LANES] = jnp.zeros((channels, LANES), low)
        ref[:, length + LANES :] = jnp.zeros((channels, LANES), low)
    mix_taps(R.mix_back, lambda g, c: pl.ds(g * square + c * group_width, group_width))
    wait(copies)

    @pl.loop(0, groups)
    def _(group):
        rows = row_block(group, group_width)
        spread_taps(R.column[rows, :].astype(f32), LANES // 2, 1, R.stage, R.taps.at[group])
        product = dot(R.mix[group], R.taps[group])
        total = product[:group_width, :length]
        for a in range(1, steps):
            part = product[a * group_width : (a + 1) * group_width, :]
            part = pltpu.roll(part, product.shape[1] - a * TAP_STEP, 1)
            total = total + part[:, :length]
        R.result[rows, :] = total.astype(low)
    pending = to_level(
        2, lambda p: R.result.at[:, lane_block(p)], R.conv_home.at[row_block(me, channels), :]
    )
    @pl.loop(0, groups)
    def _(group):
        source = R.column[row_block(group, group_width), :].astype(f32)
        span = R.shifted.shape[2]
        for a in range(steps):
            moved = pltpu.roll(source, (span + LANES - a * TAP_STEP) % (span + LANES), 1)
            R.shifted[group, a * group_width : (a + 1) * group_width, :] = moved[:, :span].astype(
                low
            )
    wait_some(seg_pending)
    clip_column(count, R.segs, R.clip)
    wait_some(brought)
    wait_some(pending)
    brought = move(34, R.cotangent, R.cotangent_home, to_level_device)

    pre = R.conv_home[...].astype(f32).T + table(0)
    share = 0.5 * (1.0 + lax.erf(pre * ROOT_HALF))
    R.slope[...] = share + pre * jnp.exp(-0.5 * pre * pre) * DENSITY_CONST
    mixed = R.frames_home[...].astype(f32) + pre * share
    R.mixed[...] = mixed
    mixed_low = mixed.astype(low)
    loads[0].wait()
    for part in range(3):
        block = dot(mixed_low, R.qkv_w[:, chunk_of(part)])
        if part != 1:
            block = block + table(1 + part // 2)
        block = block.astype(low).astype(f32)
        if part == 0:
            block = block * scale
        R.project[part] = block.T.astype(low)
    copies = to_places(
        3,
        lambda p: R.project.at[:, row_block(p, head_dim), :],
        R.main.at[:, :, lane_block(pos)],
    )
    copies += to_places(
        4,
        lambda p: R.project.at[:, row_block(count + p // 2, head_dim), :],
        R.extra.at[:, :, lane_block(pos)],
    )
    R.main[:, :, lane_block(pos)] = R.project[:, row_block(pos, head_dim), :]
    R.extra[:, :, lane_block(pos)] = R.project[:, row_block(count + pos // 2, head_dim), :]
    R.left[0] = turned(mixed_low)
    last_row = rows_count - 1

    def to_some_rows(kind, source, sends_to, comes_to):
        pending = []
        for step in range(1, rows_count):
            target = peer(row, step, rows_count)
            copy = pltpu.make_async_remote_copy(
                src_ref=source,
                dst_ref=R.late_left.at[:, lane_block(row)],
                send_sem=R.out_sem.at[kind, step],
                recv_sem=R.in_sem.at[kind, step],
                device_id={"dp": target},
                device_id_type=MESH,
            )
            sends = sends_to(target)
            pl.when(sends)(copy.start)
            pending.append((sends, comes_to, copy))
        return pending

    left_pending = to_some_rows(8, R.left.at[0], lambda p: p != last_row, row != last_row)
    wait(copies)

    size = 2 * LANES
    halves = half * LANES // size

    def scores_of(held, start, seg_row):
        scores = lax.dot_general(
            held[1], held[0, :, start], (((0,), (0,)), ((), ())), preferred_element_type=f32
        )
        return jnp.where(same_clip(R.clip, seg_row), scores, -1e30)

    def attend(held, start, index, att_ref, low_ref, lse_ref, place):
        scores = scores_of(held, start, clip_row(R.segs, index * 2, size))
        top = jnp.max(scores, axis=0, keepdims=True)
        weights = jnp.exp(scores - top)
        total = jnp.sum(weights, axis=0, keepdims=True)
        mean = dot(held[2], weights.astype(low)) / total
        att_ref[:, place] = mean
        low_ref[:, start] = mean.astype(low)
        lse_ref[:, place] = top + jnp.log(total)

    own_rows = row_block(pos, head_dim)
    extra_rows = row_block(count + pos // 2, head_dim)

    def to_half(kind, source, target_ref):
        pending = []
        for step in range(1, count):
            target, origin = peer(pos, step, count), peer(pos, count - step, count)
            copy = pltpu.make_async_remote_copy(
                src_ref=source(target),
                dst_ref=target_ref,
                send_sem=R.out_sem.at[kind, step],
                recv_sem=R.in_sem.at[kind, step],
                device_id=device_at(target, upper),
                device_id_type=MESH,
            )
            sends, comes = target // half == side, pos // half == lax.rem(origin, 2)
            pl.when(sends)(copy.start)
            pending.append((sends, comes, copy))
        return pending

    @pl.loop(0, halves)
    def _(block):
        index = side * halves + block
        place = query_span(block, size)
        attend(
            R.extra,
            query_span(index, size),
            index,
            R.att_extra,
            R.low_extra,
            R.lse_extra,
            place,
        )
    pending = to_half(5, lambda p: R.low_extra.at[:, lane_block(p)], R.att_home.at[extra_rows, :])

    @pl.when(pos // half == side)
    def _():
        R.att_home[extra_rows, :] = R.low_extra[:, lane_block(pos)]

    @pl.loop(0, length // size)
    def _(block):
        span = query_span(block, size)
        attend(R.main, span, block, R.att_main, R.low_main, R.lse_main, span)

    copies = to_places(6, lambda p: R.low_main.at[:, lane_block(p)], R.att_home.at[own_rows, :])
    R.att_home[own_rows, :] = R.low_main[:, lane_block(pos)]
    wait(copies)
    wait_some(pending)

    def to_rows(kind, source, target_ref):
        return [
            send(kind, step, source(peer(row, step, rows_count)), target_ref, target, "dp")
            for step, target in ((n, peer(row, n, rows_count)) for n in range(1, rows_count))
        ]

    def share_start(kind, part):
        own = part(row)
        return [send(kind, 2, own, own, across, "dp"), send(kind, 1, own, own, twin, "dp")]

    def share_forward(kind, part, copies):
        copies[0].wait()
        got = part(across)
        copies[0] = send(kind, 3, got, got, twin, "dp")

    def lanes_of(ref):
        return lambda index: ref.at[:, lane_block(index)]

    R.left[1] = R.att_home[...]
    att = R.att_home[...].astype(f32).T.astype(low)
    loads[1].wait()
    branch = dot(att, R.out_w[...]) + table(3)
    hidden, normed_one, inv_one = norm_forward(R.mixed[...] + branch, table(4), table(5))
    hidden_low = hidden.astype(low)
    R.hidden_all[:, lane_block(row)] = turned(hidden_low)
    hidden_copies = share_start(7, lanes_of(R.hidden_all))
    left_pending += to_some_rows(32, R.left.at[1], lambda p: p == last_row, row == last_row)
    R.late_left[:, lane_block(row)] = R.left[row // last_row]
    pieces = count // chunks
    for load in loads[2:]:
        load.wait()
    R.total[...] = hidden + table(10)

    @pl.loop(0, chunks)
    def _(chunk):
        span = query_span(chunk, width)
        pre = dot(hidden_low, R.in_w[:, span]) + R.table[pl.ds(6 + chunk, 1), :]
        share = 0.5 * (1.0 + lax.erf(pre * ROOT_HALF))
        act = (pre * share).astype(low)
        R.keep[:, span] = share + pre * jnp.exp(-0.5 * pre * pre) * DENSITY_CONST
        R.act_turned[pl.ds(chunk * pieces, pieces)] = turned(act).reshape(
            pieces, rows_count, -1, LANES
        )
        R.total[...] += dot(act, R.back_w[row_block(chunk, width), :])

    act_copies = to_rows(9, lambda p: R.act_turned.at[:, p], R.act_all.at[:, :, lane_block(row)])
    R.act_all[:, :, lane_block(row)] = R.act_turned[:, row]
    layer, normed_two, inv_two = norm_forward(R.total[...], table(11), table(12))
    R.layer_here[...] = layer.astype(low)
    layer_pending = move(35, R.layer_here, R.layer_got, from_level_device)
    wait_some(brought)
    grad_second, gain_sum, shift_sum = norm_backward(
        R.cotangent_home[...].astype(f32), normed_two, inv_two, table(11)
    )
    R.small[11, :] = gain_sum
    R.small[12, :] = shift_sum
    grad_two = grad_second.astype(low)
    R.two_all[:, lane_block(row)] = turned(grad_two)
    two_copies = share_start(10, lanes_of(R.two_all))
    R.small[10, :] = jnp.sum(grad_two.astype(f32), axis=0)
    R.total[...] = grad_second

    @pl.loop(0, chunks)
    def _(chunk):
        span = query_span(chunk, width)
        grad_pre = matmul_turned(grad_two, R.back_w[row_block(chunk, width), :]) * R.keep[:, span]
        grad_pre = grad_pre.astype(low)
        R.pre_turned[chunk] = turned(grad_pre)
        R.small[pl.ds(6 + chunk, 1), :] = jnp.sum(grad_pre.astype(f32), axis=0, keepdims=True)
        R.total[...] += matmul_turned(grad_pre, R.in_w[:, span])

    grad_first, gain_sum, shift_sum = norm_backward(R.total[...], normed_one, inv_one, table(4))
    R.small[4, :] = gain_sum
    R.small[5, :] = shift_sum
    R.mixed[...] = grad_first
    grad_branch = grad_first.astype(low)
    R.small[3, :] = jnp.sum(grad_branch.astype(f32), axis=0)
    R.turned[...] = turned(matmul_turned(grad_branch, R.out_w[...]).astype(low))

    copies = to_places(
        11, lambda p: R.turned.at[row_block(p, head_dim), :], R.gmain.at[:, lane_block(pos)]
    )
    copies += to_places(
        12,
        lambda p: R.turned.at[row_block(count + p // 2, head_dim), :],
        R.gextra.at[:, lane_block(pos)],
    )
    R.gmain[:, lane_block(pos)] = R.turned[row_block(pos, head_dim), :]
    R.gextra[:, lane_block(pos)] = R.turned[row_block(count + pos // 2, head_dim), :]
    pre_copies = to_rows(13, lambda p: R.pre_turned.at[p], R.pre_all.at[:, lane_block(row)])
    R.pre_all[:, lane_block(row)] = R.pre_turned[row]
    R.dproject[3] = turned(grad_branch)
    wait(copies)

    def attend_back(held, grads, start, index, att, lse):
        queries = held[0, :, start]
        weights = jnp.exp(scores_of(held, start, clip_row(R.segs, index * 2, size)) - lse)
        grad_prob = lax.dot_general(
            held[2], grads, (((0,), (0,)), ((), ())), preferred_element_type=f32
        )
        delta = jnp.sum(grads.astype(f32) * att, axis=0, keepdims=True)
        grad_score = (weights * (grad_prob - delta)).astype(low)
        return (
            dot(held[1], grad_score) * scale,
            matmul_turned(queries, grad_score),
            matmul_turned(grads, weights.astype(low)),
        )

    R.dkey[...] = jnp.zeros_like(R.dkey)
    R.dvalue[...] = jnp.zeros_like(R.dvalue)

    @pl.loop(0, halves)
    def _(block):
        index = side * halves + block
        span = query_span(index, size)
        place = query_span(block, size)
        parts = attend_back(
            R.extra, R.gextra[:, span], span, index, R.att_extra[:, place], R.lse_extra[:, place]
        )
        R.dextra[0, :, span] = parts[0].astype(low)
        R.dkey[...] += parts[1]
        R.dvalue[...] += parts[2]

    R.dextra[1] = R.dkey[...].astype(low)
    R.dextra[2] = R.dvalue[...].astype(low)
    part_rows = row_block(pos // 2, head_dim)
    copies = to_places(
        14, lambda p: R.dextra.at[1:3, :, lane_block(p)], R.halves.at[side, :, part_rows, :]
    )
    pending = to_half(
        15, lambda p: R.dextra.at[0, :, lane_block(p)], R.dproject.at[0, extra_rows, :]
    )
    R.halves[side, :, part_rows, :] = R.dextra[1:3, :, lane_block(pos)]

    @pl.when(pos // half == side)
    def _():
        R.dproject[0, extra_rows, :] = R.dextra[0, :, lane_block(pos)]

    lower = lax.rem(level, 2)
    level_mate = me + 2 - 4 * lower
    upper_mate = me + 4 - 8 * upper

    def shard(u, bit, other, side_first):
        return row_block(4 * u + (2 * other + bit if side_first else 2 * bit + other), channels)

    def sum_begin(kind, slot, source, span, side_first):
        bit, mate = (side, near) if side_first else (lower, level_mate)
        return [
            send(
                kind,
                2 * u + v,
                R.in_w.at[shard(u, 1 - bit, v, side_first), source],
                R.got_one.at[slot, 2 * u + v, :, span],
                mate,
            )
            for u in range(2)
            for v in range(2)
        ]

    def sum_next(kind, slot, source, span, side_first, copies):
        wait(copies)
        bit, other = (side, lower) if side_first else (lower, side)
        mate = level_mate if side_first else near
        for u in range(2):
            for v in range(2):
                own = R.in_w[shard(u, bit, v, side_first), source]
                got = R.got_one[slot, 2 * u + v, :, span]
                R.sum_one[slot, 2 * u + v, :, span] = (own.astype(f32) + got.astype(f32)).astype(
                    low
                )
        return [
            send(
                kind,
                u,
                R.sum_one.at[slot, 2 * u + 1 - other, :, span],
                R.got_two.at[slot, u, :, span],
                mate,
            )
            for u in range(2)
        ]

    def sum_last(kind, slot, span, side_first, copies):
        wait(copies)
        other = lower if side_first else side
        for u in range(2):
            own = R.sum_one[slot, 2 * u + other, :, span]
            got = R.got_two[slot, u, :, span]
            R.sum_two[slot, u, :, span] = (own.astype(f32) + got.astype(f32)).astype(low)
        return [
            send(
                kind,
                0,
                R.sum_two.at[slot, 1 - upper, :, span],
                R.got_three.at[slot, :, span],
                upper_mate,
            )
        ]

    def summed(slot, copies):
        wait(copies)
        return (R.sum_two[slot, upper].astype(f32) + R.got_three[slot].astype(f32)).astype(low)

    every = slice(0, width)
    in_span, out_span = chunk_of(0), chunk_of(1)
    stores = []

    def store(index, source, target):
        copy = pltpu.make_async_copy(source, target, R.store_sem.at[index])
        copy.start()
        stores.append(copy)

    share_forward(10, lanes_of(R.two_all), two_copies)
    share_forward(7, lanes_of(R.hidden_all), hidden_copies)
    blocks = length // size

    def main_back(block):
        span = query_span(block, size)
        parts = attend_back(
            R.main, R.gmain[:, span], span, block, R.att_main[:, span], R.lse_main[:, span]
        )
        R.dmain[0, :, span] = parts[0].astype(low)
        R.dkey[...] += parts[1]
        R.dvalue[...] += parts[2]

    R.dkey[...] = jnp.zeros_like(R.dkey)
    R.dvalue[...] = jnp.zeros_like(R.dvalue)
    pl.loop(0, blocks // 2)(main_back)
    wait(two_copies)
    wait(act_copies)
    product = matmul_turned(R.act_all[...].reshape(width, -1), R.two_all[...])
    R.in_w[:, out_span] = product.astype(low)
    out_copies = sum_begin(18, 1, out_span, every, False)
    pl.loop(blocks // 2, blocks)(main_back)
    R.dmain[1] = R.dkey[...].astype(low)
    R.dmain[2] = R.dvalue[...].astype(low)
    copies += to_places(
        16, lambda p: R.dmain.at[:, :, lane_block(p)], R.dproject.at[0:3, own_rows, :]
    )
    R.dproject[0:3, own_rows, :] = R.dmain[:, :, lane_block(pos)]
    wait(hidden_copies)
    wait(pre_copies)
    R.in_w[:, in_span] = matmul_turned(R.hidden_all[...], R.pre_all[...]).astype(low)
    in_copies = sum_begin(17, 0, in_span, every, True)
    wait(copies)
    wait_some(pending)
    first = half * head_dim
    for which in range(2):
        total = R.halves[0, which].astype(f32) + R.halves[1, which].astype(f32)
        R.dproject[1 + which, width - first :, :] = total.astype(low)

    late = to_rows(19, lambda p: R.dproject.at[p], R.late_right.at[:, lane_block(row)])
    R.late_right[:, lane_block(row)] = R.dproject[row]
    grad_mixed = R.mixed[...]
    for part in range(3):
        block = R.dproject[part].astype(f32).T
        if part != 1:
            R.small[1 + part // 2, :] = jnp.sum(block, axis=0)
        grad_mixed = grad_mixed + matmul_turned(block.astype(low), R.qkv_w[:, chunk_of(part)])
    R.mixed_here[...] = grad_mixed.astype(low)
    grad_conv = (grad_mixed * R.slope[...]).astype(low)
    R.conv_turned[...] = turned(grad_conv)
    conv_pending = from_level(
        20, lambda b: R.conv_turned.at[row_block(b, channels), :], R.gcol.at[:, lane_block(pos + 1)]
    )
    R.small[0, :] = jnp.sum(grad_conv.astype(f32), axis=0)
    small_copy = send(21, 0, R.small, R.small_got.at[0], twin, "dp")
    out_copies = sum_next(23, 1, out_span, every, False, out_copies)
    in_copies = sum_next(22, 0, in_span, every, True, in_copies)
    mixed_pending = move(36, R.mixed_here, R.mixed_got, from_level_device)
    wait_some(conv_pending)
    @pl.loop(0, groups)
    def _(group):
        rows = row_block(group, group_width)
        spread_taps(R.gcol[rows, :].astype(f32), LANES // 2, -1, R.stage, R.taps.at[group])
        product = dot(R.mix_back[group], R.taps[group])
        total = product[:group_width, LANES:]
        for a in range(1, steps):
            part = product[a * group_width : (a + 1) * group_width, :]
            total = total + pltpu.roll(part, a * TAP_STEP, 1)[:, LANES:]
        R.result[rows, :] = total.astype(low)
    back = to_blocks(
        24, lambda p: R.result.at[:, lane_block(p)], R.back_home.at[row_block(me, channels), :]
    )
    R.back_home[row_block(me, channels), :] = R.result[:, lane_block(me)]

    wait(late)
    wait_some(left_pending)
    product = matmul_turned(R.late_left[...], R.late_right[...])
    R.in_w[:, chunk_of(2)] = product.astype(low)
    middle = width // 2
    parts = (
        (26, slice(2 * width, 2 * width + middle), slice(0, middle), True),
        (28, slice(2 * width + middle, 3 * width), slice(middle, width), False),
    )
    att_copies = [sum_begin(kind, 2, source, span, first) for kind, source, span, first in parts]
    out_copies = sum_last(37, 1, every, False, out_copies)
    quarter = channels // rows_count
    @pl.loop(0, groups)
    def _(group):
        grad = matmul_turned(R.shifted[group], R.taps[group])
        for block in range(group_width // steps):
            span = slice(block * LANES, (block + 1) * LANES)
            tiles = [
                grad[a * group_width : (a + 1) * group_width, span] for a in range(steps)
            ]
            for u, tile in enumerate(swap_blocks(tiles, TAP_STEP)):
                channel = block * steps + u
                R.conv_part[group, channel // quarter, channel % quarter] = tile.astype(low)
    conv_copy = send(25, 0, R.conv_part.at[:, 1 - core], R.conv_got, twin, "dp")
    small_copy.wait()
    R.small_sum[0] = R.small[...] + R.small_got[0]
    small_copy = send(21, 1, R.small_sum.at[0], R.small_got.at[1], across, "dp")
    in_copies = sum_last(38, 0, every, True, in_copies)
    att_copies = [
        sum_next(kind + 1, 2, source, span, first, copies)
        for (kind, source, span, first), copies in zip(parts, att_copies)
    ]
    conv_copy.wait()
    for part in range(2):
        R.conv_sum[part] = (
            R.conv_part[part, core].astype(f32) + R.conv_got[part].astype(f32)
        ).astype(low)
    conv_copy = send(25, 1, R.conv_sum.at[1 - row // 2], R.conv_far, across, "dp")
    small_copy.wait()
    R.small_sum[1] = R.small_sum[0] + R.small_got[1]
    small_copy = send(21, 2, R.small_sum.at[1], R.small_got.at[2], near)

    def slots_of(ref):
        return lambda index: ref.at[index]

    def part_of(ref, which):
        return lambda index: ref.at[index, which]

    R.ffn_sums[row, 1] = summed(1, out_copies)
    out_share = share_start(43, part_of(R.ffn_sums, 1))
    R.ffn_sums[row, 0] = summed(0, in_copies)
    in_share = share_start(40, part_of(R.ffn_sums, 0))
    att_copies = [
        sum_last(kind + 13, 2, span, first, copies)
        for (kind, source, span, first), copies in zip(parts, att_copies)
    ]
    wait(back)
    wait_some(mixed_pending)
    R.frames_done[...] = (
        R.mixed_got[...].astype(f32) + (R.back_home[...].astype(f32) * valid).T
    ).astype(low)
    store(0, R.frames_done, R.frames_out)
    wait_some(layer_pending)
    store(1, R.layer_got, R.layer_out)
    conv_copy.wait()
    R.conv_sums[row] = (
        R.conv_sum[row // 2].astype(f32) + R.conv_far[...].astype(f32)
    ).astype(low)
    conv_share = share_start(42, slots_of(R.conv_sums))
    small_copy.wait()
    R.small_far[level] = R.small_sum[1] + R.small_got[2]
    smalls = []
    for step in range(1, levels):
        target = 2 * peer(level, step, levels) + side
        smalls.append(
            send(30, step, R.small_far.at[level], R.small_far.at[level], target)
        )
    share_forward(43, part_of(R.ffn_sums, 1), out_share)
    share_forward(40, part_of(R.ffn_sums, 0), in_share)
    R.attn_sums[row] = summed(2, att_copies[0] + att_copies[1])
    att_share = share_start(31, slots_of(R.attn_sums))
    share_forward(42, slots_of(R.conv_sums), conv_share)
    wait(smalls)
    R.small_done[...] = sum_parts(R.small_far)
    store(2, R.small_done, R.small_out)
    wait(out_share)
    wait(in_share)
    store(3, R.ffn_sums, R.ffn_out)
    wait(conv_share)
    store(4, R.conv_sums, R.conv_out)
    share_forward(31, slots_of(R.attn_sums), att_share)
    wait(att_share)
    store(5, R.attn_sums, R.attn_out)
    for copy in stores:
        copy.wait()


VECTORS = (
    "conv_bias",
    "qv_bias",
    "out_bias",
    "gain_one",
    "shift_one",
    "in_bias",
    "back_bias",
    "gain_two",
    "shift_two",
)


def layer(count, rows_count, head_dim, named):
    low, f32 = jnp.bfloat16, jnp.float32
    tokens, width = named["frames"].shape
    wide = named["in_hbm"].shape[1]
    _, group_width, kernel = named["conv_hbm"].shape
    channels = width // count
    groups = channels // group_width
    length = count * LANES
    span = length + LANES
    steps = kernel // TAP_STEP
    taps = group_width * TAP_STEP
    every = rows_count * tokens
    piece = channels // rows_count
    extras = count // 2 * head_dim
    levels = count // 2
    outs = {
        "layer_out": ((tokens, width), low),
        "frames_out": ((tokens, width), low),
        "conv_out": ((rows_count, piece, group_width, kernel), low),
        "ffn_out": ((rows_count, 2, channels, width), low),
        "attn_out": ((rows_count, channels, width), low),
        "small_out": ((16, width), f32),
    }
    scratch = {
        "qkv_w": (named["qkv_hbm"].shape, low),
        "out_w": (named["out_hbm"].shape, low),
        "in_w": (named["in_hbm"].shape, low),
        "back_w": (named["back_hbm"].shape, low),
        "table": ((16, width), f32),
        "small": ((16, width), f32),
        "small_got": ((3, 16, width), f32),
        "small_sum": ((2, 16, width), f32),
        "small_far": ((levels, 16, width), f32),
        "turned": ((width, tokens), low),
        "conv_turned": ((width, tokens), low),
        "column": ((channels, span + LANES), low),
        "gcol": ((channels, span + LANES), low),
        "segs": ((count, 1, LANES), jnp.int32),
        "clip": ((length, LANES), f32),
        "stage": ((span // LANES * taps, LANES), f32),
        "own_weight": ((channels, group_width, kernel), low),
        "frames_home": ((tokens, width), low),
        "cotangent_home": ((tokens, width), low),
        "layer_here": ((tokens, width), low),
        "mixed_here": ((tokens, width), low),
        "mixed_got": ((tokens, width), low),
        "taps": ((groups, taps, span), low),
        "mix": ((groups, steps * group_width, taps), low),
        "mix_back": ((groups, steps * group_width, taps), low),
        "shifted": ((groups, steps * group_width, span), low),
        "result": ((channels, length), low),
        "conv_home": ((width, tokens), low),
        "back_home": ((width, tokens), low),
        "slope": ((tokens, width), f32),
        "mixed": ((tokens, width), f32),
        "project": ((3, width, tokens), low),
        "main": ((3, head_dim, length), low),
        "extra": ((3, head_dim, length), low),
        "att_main": ((head_dim, length), f32),
        "att_extra": ((head_dim, length // 2), f32),
        "low_main": ((head_dim, length), low),
        "low_extra": ((head_dim, length), low),
        "lse_main": ((1, length), f32),
        "lse_extra": ((1, length // 2), f32),
        "att_home": ((width, tokens), low),
        "keep": ((tokens, wide), f32),
        "total": ((tokens, width), f32),
        "dkey": ((head_dim, length), f32),
        "dvalue": ((head_dim, length), f32),
        "left": ((2, width, tokens), low),
        "act_turned": ((count, rows_count, wide // (count * rows_count), tokens), low),
        "pre_turned": ((rows_count, width, tokens), low),
        "hidden_all": ((width, every), low),
        "two_all": ((width, every), low),
        "pre_all": ((width, every), low),
        "act_all": ((count, wide // (count * rows_count), every), low),
        "late_left": ((width, every), low),
        "late_right": ((width, every), low),
        "gmain": ((head_dim, length), low),
        "gextra": ((head_dim, length), low),
        "dmain": ((3, head_dim, length), low),
        "dextra": ((3, head_dim, length), low),
        "dproject": ((4, width, tokens), low),
        "halves": ((2, 2, extras, tokens), low),
        "got_one": ((3, 4, channels, width), low),
        "sum_one": ((3, 4, channels, width), low),
        "got_two": ((3, 2, channels, width), low),
        "sum_two": ((3, 2, channels, width), low),
        "got_three": ((3, channels, width), low),
        "layer_got": ((tokens, width), low),
        "frames_done": ((tokens, width), low),
        "small_done": ((16, width), f32),
        "ffn_sums": ((rows_count, 2, channels, width), low),
        "conv_sums": ((rows_count, piece, group_width, kernel), low),
        "attn_sums": ((rows_count, channels, width), low),
        "conv_part": ((2, 2, piece, group_width, kernel), low),
        "conv_got": ((2, piece, group_width, kernel), low),
        "conv_sum": ((2, piece, group_width, kernel), low),
        "conv_far": ((piece, group_width, kernel), low),
    }
    hbm = pl.BlockSpec(memory_space=pl.ANY)
    names = (*named, *outs, *scratch, "out_sem", "in_sem", "load_sem", "store_sem")
    return pl.pallas_call(
        functools.partial(layer_kernel, names, count, rows_count, head_dim),
        out_shape=tuple(jax.ShapeDtypeStruct(*out) for out in outs.values()),
        in_specs=[hbm if name.endswith("_hbm") else VMEM for name in named],
        out_specs=(hbm,) * len(outs),
        scratch_shapes=[pltpu.VMEM(*item) for item in scratch.values()]
        + [
            pltpu.SemaphoreType.DMA((44, count)),
            pltpu.SemaphoreType.DMA((44, count)),
            pltpu.SemaphoreType.DMA((3 + 2 * (wide // width),)),
            pltpu.SemaphoreType.DMA((len(outs),)),
        ],
        compiler_params=pltpu.CompilerParams(
            collective_id=0, has_side_effects=True, vmem_limit_bytes=62 * 2**20
        ),
        name="layer",
    )(*named.values())


def unpack_kernel(
    count,
    layer_hbm,
    frames_hbm,
    conv_hbm,
    ffn_hbm,
    attn_hbm,
    small_hbm,
    layer_out,
    frames_out,
    conv_out,
    conv_bias,
    qkv_out,
    qv_bias,
    out_out,
    out_bias,
    gain_one,
    shift_one,
    in_out,
    in_bias,
    back_out,
    back_bias,
    gain_two,
    shift_two,
    conv_wide,
    qkv_wide,
    out_wide,
    in_wide,
    back_wide,
    conv_ref,
    ffn_ref,
    attn_ref,
    small_ref,
    layer_ref,
    frames_ref,
    spare,
    sems,
):
    f32 = jnp.float32
    me = lax.axis_index("blk")
    rows_count, channels, width = attn_ref.shape
    piece = conv_ref.shape[1]
    copies = []

    def start(source, target):
        copy = pltpu.make_async_copy(source, target, sems.at[len(copies)])
        copy.start()
        copies.append(copy)

    loads = [
        pltpu.make_async_copy(source, target, sems.at[6 + rows_count + i])
        for i, (source, target) in enumerate(
            (
                (conv_hbm, conv_ref),
                (ffn_hbm, ffn_ref),
                (attn_hbm, attn_ref),
                (small_hbm, small_ref),
                (layer_hbm, layer_ref),
                (frames_hbm, frames_ref),
            )
        )
    ]
    for load in loads:
        load.start()
    loads[0].wait()
    for row in range(rows_count):
        part = slice(row * piece, (row + 1) * piece)
        conv_wide[part] = conv_ref[row].astype(f32)
        start(conv_wide.at[part], conv_out.at[part])
    loads[1].wait()
    loads[2].wait()
    for row in range(rows_count):
        part = slice(row * channels, (row + 1) * channels)
        span = slice(row * width, (row + 1) * width)
        in_wide[:, span] = ffn_ref[row, 0].astype(f32)
        back_wide[part, :] = ffn_ref[row, 1].astype(f32)
        if row < rows_count - 1:
            qkv_wide[:, span] = attn_ref[row].astype(f32)
        else:
            out_wide[...] = attn_ref[row].astype(f32)
    start(in_wide, in_out)
    start(back_wide, back_out)
    start(qkv_wide, qkv_out)
    start(out_wide, out_out)
    loads[4].wait()
    start(layer_ref, layer_out)
    loads[5].wait()
    start(frames_ref, frames_out)
    loads[3].wait()
    small = small_ref[...]
    own = pltpu.roll(small, lax.rem(width - channels * me, width), 1)
    for place, ref in (
        (0, conv_bias),
        (3, out_bias),
        (4, gain_one),
        (5, shift_one),
        (10, back_bias),
        (11, gain_two),
        (12, shift_two),
    ):
        ref[...] = own[place, :channels]
    for first, parts, ref in ((1, 2, qv_bias), (6, rows_count, in_bias)):
        size = parts * channels
        inside = count // parts
        spare[...] = pltpu.roll(small, lax.rem(width - size * lax.rem(me, inside), width), 1)
        ref[...] = spare[pl.ds(first + me // inside, 1), :][0, :size]
    for copy in copies:
        copy.wait()


def unpack(count, layer_out, frames_out, conv, ffn, attn, small):
    rows_count, channels, width = attn.shape
    piece, group_width, kernel = conv.shape[1:]
    f32 = jnp.float32
    hbm = pl.BlockSpec(memory_space=pl.ANY)
    vector = jax.ShapeDtypeStruct((channels,), f32)
    conv_type = jax.ShapeDtypeStruct((rows_count * piece, group_width, kernel), f32)
    qkv_type = jax.ShapeDtypeStruct((channels, (rows_count - 1) * width), f32)
    out_type = jax.ShapeDtypeStruct((channels, width), f32)
    in_type = jax.ShapeDtypeStruct((channels, rows_count * width), f32)
    back_type = jax.ShapeDtypeStruct((rows_count * channels, width), f32)
    results = pl.pallas_call(
        functools.partial(unpack_kernel, count),
        out_shape=(
            jax.ShapeDtypeStruct(layer_out.shape, layer_out.dtype),
            jax.ShapeDtypeStruct(frames_out.shape, frames_out.dtype),
            conv_type,
            vector,
            qkv_type,
            jax.ShapeDtypeStruct((2 * channels,), f32),
            out_type,
            vector,
            vector,
            vector,
            in_type,
            jax.ShapeDtypeStruct((rows_count * channels,), f32),
            back_type,
            vector,
            vector,
            vector,
        ),
        in_specs=[hbm] * 6,
        out_specs=(
            hbm,
            hbm,
            hbm,
            VMEM,
            hbm,
            VMEM,
            hbm,
            VMEM,
            VMEM,
            VMEM,
            hbm,
            VMEM,
            hbm,
            VMEM,
            VMEM,
            VMEM,
        ),
        scratch_shapes=[
            pltpu.VMEM(item.shape, f32)
            for item in (conv_type, qkv_type, out_type, in_type, back_type)
        ]
        + [pltpu.VMEM(item.shape, item.dtype) for item in (conv, ffn, attn, small, layer_out, frames_out)]
        + [pltpu.VMEM(small.shape, f32), pltpu.SemaphoreType.DMA((12 + rows_count,))],
        compiler_params=pltpu.CompilerParams(vmem_limit_bytes=62 * 2**20),
        name="unpack",
    )(layer_out, frames_out, conv, ffn, attn, small)
    return (results[0][None], results[1][None], *results[2:])


def shards(sizes, *arrays):
    frames, segment, conv_weight = arrays[:3]
    row_count, block_len, model_width = frames.shape
    group_width, kernel = conv_weight.shape[1:]
    count = sizes["blk"]
    head_dim = model_width // HEADS
    channels = model_width // count
    fits = (
        row_count == 1
        and block_len == LANES
        and kernel == LANES
        and channels % group_width == 0
        and group_width % TAP_STEP == 0
        and count % 4 == 0
        and 2 * HEADS == 3 * count
        and head_dim % TAP_STEP == 0
        and sizes["dp"] == 4
        and count % sizes["dp"] == 0
        and arrays[10].shape[1] == 4 * model_width
    )
    if fits:
        return swap_shards(count, sizes["dp"], *arrays)
    return ring_shards(*arrays)


def swap_shards(
    count,
    rows_count,
    frames,
    segment,
    conv_weight,
    conv_bias,
    qkv_weight,
    qv_bias,
    out_weight,
    out_bias,
    norm1_gain,
    norm1_bias,
    ffn_in,
    ffn_in_bias,
    ffn_out,
    ffn_out_bias,
    norm2_gain,
    norm2_bias,
    cotangent,
):
    named = {
        "frames": frames[0],
        "segment": segment,
        "cotangent": cotangent[0],
        "conv_bias": conv_bias,
        "qv_bias": qv_bias,
        "out_bias": out_bias,
        "gain_one": norm1_gain,
        "shift_one": norm1_bias,
        "in_bias": ffn_in_bias,
        "back_bias": ffn_out_bias,
        "gain_two": norm2_gain,
        "shift_two": norm2_bias,
        "conv_hbm": conv_weight,
        "qkv_hbm": qkv_weight,
        "out_hbm": out_weight,
        "in_hbm": ffn_in,
        "back_hbm": ffn_out,
    }
    width = frames.shape[2]
    results = layer(count, rows_count, width // HEADS, named)
    return unpack(count, *results)


def solution(mesh):
    return jax.shard_map(
        functools.partial(shards, mesh.shape),
        mesh=mesh,
        in_specs=(
            P("dp", "blk", None),
            P("dp", "blk"),
            P(),
            P(),
            P(),
            P(),
            P(),
            P(),
            P(),
            P(),
            P(),
            P(),
            P(),
            P(),
            P(),
            P(),
            P("dp", "blk", None),
        ),
        out_specs=(
            P("dp", "blk", None),
            P("dp", "blk", None),
            P("blk", None, None),
            P("blk"),
            P("blk", None),
            P("blk"),
            P("blk", None),
            P("blk"),
            P("blk"),
            P("blk"),
            P("blk", None),
            P("blk"),
            P("blk", None),
            P("blk"),
            P("blk"),
            P("blk"),
        ),
        check_vma=False,
    )
```

profile of v0, /device:TPU:0, one launch (start us, length us, event | category | flops | bytes accessed | tf_op | source)
XLA Modules:
  0.0 164.9 jit_solution(15755047858369524549)
XLA Ops:
  0.7 159.4 %layer.1 = (bf16[128,768]{1,0:T(8,128)(2,1)}, bf16[128,768]{1,0:T(8,128)(2,1)}, bf16[4,24,48,128]{3,2,1,0:T(8,128)(2,1)}, bf16[4,2,96,768]{3,2,1,0:T(8,128)(2,1)...) custom-call(bf16[128,768]{1,0:T(8,128)(2,1)} %bitcast.4, s32[1,128]{1,0:T(1,128)} %refs_1_.1, bf16[128,768]{1,0:T(8,128)(2,1)} %bitcast.5, ...), custom_call_target="tpu_custom_call" | custom-call | tf_op jit(solution)/shard_map/layer/pallas_call | solution.py:1344
  160.1 4.7 %unpack.1 = (bf16[128,768]{1,0:T(8,128)(2,1)}, bf16[128,768]{1,0:T(8,128)(2,1)}, f32[96,48,128]{2,1,0:T(8,128)}, f32[96]{0:T(128)}, f32[96,2304]{1,0:T(8,128)}, ...) custom-call(bf16[128,768]{1,0:T(8,128)(2,1)} %get-tuple-element.38.l, ...), custom_call_target="tpu_custom_call" | custom-call | tf_op jit(solution)/shard_map/unpack/pallas_call | solution.py:1484
where the time goes:
time: 165 us
  Pallas kernels  164 us (99%)
    pallas_call x1, Pallas kernels, layer(): pl.pallas_call(functools.partial(layer_kernel, names, count, rows_count,...  159 us
    pallas_call x1, Pallas kernels, unpack(): pl.pallas_call(functools.partial(unpack_kernel, count), out_shape=(jax.Sh...  4.68 us

commit v1 on v0

--- a/solution.py
+++ b/solution.py
@@ -531,6 +531,9 @@
     pos = 4 * core + 2 * lax.rem(level, 2) + side
     home_row = 2 * (row // 2) + upper
     at_home = core == upper
+    east = row // 2
+    corner = 2 * side + core
+    facing = peer(corner, 2, 4)
     across = peer(row, 2, rows_count)
     tokens, width = R.frames.shape
     channels = width // count
@@ -741,15 +744,15 @@
         if part == 0:
             block = block * scale
         R.project[part] = block.T.astype(low)
+    extra_copies = to_places(
+        4,
+        lambda p: R.project.at[:, row_block(count + p // 2, head_dim), :],
+        R.extra.at[:, :, lane_block(pos)],
+    )
     copies = to_places(
         3,
         lambda p: R.project.at[:, row_block(p, head_dim), :],
         R.main.at[:, :, lane_block(pos)],
-    )
-    copies += to_places(
-        4,
-        lambda p: R.project.at[:, row_block(count + p // 2, head_dim), :],
-        R.extra.at[:, :, lane_block(pos)],
     )
     R.main[:, :, lane_block(pos)] = R.project[:, row_block(pos, head_dim), :]
     R.extra[:, :, lane_block(pos)] = R.project[:, row_block(count + pos // 2, head_dim), :]
@@ -774,7 +777,7 @@
         return pending
 
     left_pending = to_some_rows(8, R.left.at[0], lambda p: p != last_row, row != last_row)
-    wait(copies)
+    wait(extra_copies)
 
     size = 2 * LANES
     halves = half * LANES // size
@@ -834,6 +837,8 @@
     def _():
         R.att_home[extra_rows, :] = R.low_extra[:, lane_block(pos)]
 
+    wait(copies)
+
     @pl.loop(0, length // size)
     def _(block):
         span = query_span(block, size)
@@ -850,13 +855,13 @@
             for step, target in ((n, peer(row, n, rows_count)) for n in range(1, rows_count))
         ]
 
-    def share_start(kind, part):
-        own = part(row)
-        return [send(kind, 2, own, own, across, "dp"), send(kind, 1, own, own, twin, "dp")]
-
-    def share_forward(kind, part, copies):
+    def share_start(kind, part, index=row, mate={"dp": across}):
+        own = part(index)
+        return [send(kind, 2, own, own, mate), send(kind, 1, own, own, twin, "dp")]
+
+    def share_forward(kind, part, copies, index=across):
         copies[0].wait()
-        got = part(across)
+        got = part(index)
         copies[0] = send(kind, 3, got, got, twin, "dp")
 
     def lanes_of(ref):
@@ -868,8 +873,8 @@
     branch = dot(att, R.out_w[...]) + table(3)
     hidden, normed_one, inv_one = norm_forward(R.mixed[...] + branch, table(4), table(5))
     hidden_low = hidden.astype(low)
-    R.hidden_all[:, lane_block(row)] = turned(hidden_low)
-    hidden_copies = share_start(7, lanes_of(R.hidden_all))
+    R.hidden_all[:, lane_block(corner)] = turned(hidden_low)
+    hidden_copies = share_start(7, lanes_of(R.hidden_all), corner, {"blk": near})
     left_pending += to_some_rows(32, R.left.at[1], lambda p: p == last_row, row == last_row)
     R.late_left[:, lane_block(row)] = R.left[row // last_row]
     pieces = count // chunks
@@ -923,20 +928,26 @@
     R.small[3, :] = jnp.sum(grad_branch.astype(f32), axis=0)
     R.turned[...] = turned(matmul_turned(grad_branch, R.out_w[...]).astype(low))
 
-    copies = to_places(
-        11, lambda p: R.turned.at[row_block(p, head_dim), :], R.gmain.at[:, lane_block(pos)]
-    )
-    copies += to_places(
+    extra_copies = to_places(
         12,
         lambda p: R.turned.at[row_block(count + p // 2, head_dim), :],
         R.gextra.at[:, lane_block(pos)],
     )
+    copies = to_places(
+        11, lambda p: R.turned.at[row_block(p, head_dim), :], R.gmain.at[:, lane_block(pos)]
+    )
     R.gmain[:, lane_block(pos)] = R.turned[row_block(pos, head_dim), :]
     R.gextra[:, lane_block(pos)] = R.turned[row_block(count + pos // 2, head_dim), :]
-    pre_copies = to_rows(13, lambda p: R.pre_turned.at[p], R.pre_all.at[:, lane_block(row)])
-    R.pre_all[:, lane_block(row)] = R.pre_turned[row]
+    pre_copies = []
+    for step in range(1, 4):
+        target = peer(corner, step, 4)
+        device = {"dp": 2 * east + lax.rem(target, 2), "blk": 2 * level + target // 2}
+        pre_copies.append(
+            send(13, step, R.pre_turned.at[target], R.pre_all.at[:, lane_block(corner)], device)
+        )
+    R.pre_all[:, lane_block(corner)] = R.pre_turned[corner]
     R.dproject[3] = turned(grad_branch)
-    wait(copies)
+    wait(extra_copies)
 
     def attend_back(held, grads, start, index, att, lse):
         queries = held[0, :, start]
@@ -970,6 +981,7 @@
     R.dextra[1] = R.dkey[...].astype(low)
     R.dextra[2] = R.dvalue[...].astype(low)
     part_rows = row_block(pos // 2, head_dim)
+    wait(copies)
     copies = to_places(
         14, lambda p: R.dextra.at[1:3, :, lane_block(p)], R.halves.at[side, :, part_rows, :]
     )
@@ -986,16 +998,22 @@
     level_mate = me + 2 - 4 * lower
     upper_mate = me + 4 - 8 * upper
 
-    def shard(u, bit, other, side_first):
-        return row_block(4 * u + (2 * other + bit if side_first else 2 * bit + other), channels)
-
-    def sum_begin(kind, slot, source, span, side_first):
-        bit, mate = (side, near) if side_first else (lower, level_mate)
+    modes = {
+        "side": (side, {"blk": near}, lower, {"blk": level_mate}),
+        "east": (east, {"dp": across}, lower, {"blk": level_mate}),
+        "level": (lower, {"blk": level_mate}, side, {"blk": near}),
+    }
+
+    def shard(u, bit, other, mode):
+        return row_block(4 * u + (2 * bit + other if mode == "level" else 2 * other + bit), channels)
+
+    def sum_begin(kind, slot, source, span, mode):
+        bit, mate, _, _ = modes[mode]
         return [
             send(
                 kind,
                 2 * u + v,
-                R.in_w.at[shard(u, 1 - bit, v, side_first), source],
+                R.in_w.at[shard(u, 1 - bit, v, mode), source],
                 R.got_one.at[slot, 2 * u + v, :, span],
                 mate,
             )
@@ -1003,13 +1021,12 @@
             for v in range(2)
         ]
 
-    def sum_next(kind, slot, source, span, side_first, copies):
+    def sum_next(kind, slot, source, span, mode, copies):
         wait(copies)
-        bit, other = (side, lower) if side_first else (lower, side)
-        mate = level_mate if side_first else near
+        bit, _, other, mate = modes[mode]
         for u in range(2):
             for v in range(2):
-                own = R.in_w[shard(u, bit, v, side_first), source]
+                own = R.in_w[shard(u, bit, v, mode), source]
                 got = R.got_one[slot, 2 * u + v, :, span]
                 R.sum_one[slot, 2 * u + v, :, span] = (own.astype(f32) + got.astype(f32)).astype(
                     low
@@ -1025,9 +1042,9 @@
             for u in range(2)
         ]
 
-    def sum_last(kind, slot, span, side_first, copies):
+    def sum_last(kind, slot, span, mode, copies):
         wait(copies)
-        other = lower if side_first else side
+        other = modes[mode][2]
         for u in range(2):
             own = R.sum_one[slot, 2 * u + other, :, span]
             got = R.got_two[slot, u, :, span]
@@ -1056,7 +1073,7 @@
         stores.append(copy)
 
     share_forward(10, lanes_of(R.two_all), two_copies)
-    share_forward(7, lanes_of(R.hidden_all), hidden_copies)
+    share_forward(7, lanes_of(R.hidden_all), hidden_copies, facing)
     blocks = length // size
 
     def main_back(block):
@@ -1065,8 +1082,22 @@
             R.main, R.gmain[:, span], span, block, R.att_main[:, span], R.lse_main[:, span]
         )
         R.dmain[0, :, span] = parts[0].astype(low)
+        for place in range(size // LANES):
+            target = block * (size // LANES) + place
+            pl.when(target != pos)(query_copy(target).start)
         R.dkey[...] += parts[1]
         R.dvalue[...] += parts[2]
+
+    def query_copy(target):
+        step = lax.rem(target - pos + count, count)
+        return pltpu.make_async_remote_copy(
+            src_ref=R.dmain.at[0, :, lane_block(target)],
+            dst_ref=R.dproject.at[0, own_rows, :],
+            send_sem=R.out_sem.at[16, step],
+            recv_sem=R.in_sem.at[16, step],
+            device_id=device_at(target, upper),
+            device_id_type=MESH,
+        )
 
     R.dkey[...] = jnp.zeros_like(R.dkey)
     R.dvalue[...] = jnp.zeros_like(R.dvalue)
@@ -1075,18 +1106,20 @@
     wait(act_copies)
     product = matmul_turned(R.act_all[...].reshape(width, -1), R.two_all[...])
     R.in_w[:, out_span] = product.astype(low)
-    out_copies = sum_begin(18, 1, out_span, every, False)
+    out_copies = sum_begin(18, 1, out_span, every, "level")
+    wait(hidden_copies)
+    wait(pre_copies)
+    R.in_w[:, in_span] = matmul_turned(R.hidden_all[...], R.pre_all[...]).astype(low)
+    in_copies = sum_begin(17, 0, in_span, every, "east")
     pl.loop(blocks // 2, blocks)(main_back)
     R.dmain[1] = R.dkey[...].astype(low)
     R.dmain[2] = R.dvalue[...].astype(low)
     copies += to_places(
-        16, lambda p: R.dmain.at[:, :, lane_block(p)], R.dproject.at[0:3, own_rows, :]
-    )
+        44, lambda p: R.dmain.at[1:3, :, lane_block(p)], R.dproject.at[1:3, own_rows, :]
+    )
+    copies += [query_copy(peer(pos, step, count)) for step in range(1, count)]
     R.dproject[0:3, own_rows, :] = R.dmain[:, :, lane_block(pos)]
-    wait(hidden_copies)
-    wait(pre_copies)
-    R.in_w[:, in_span] = matmul_turned(R.hidden_all[...], R.pre_all[...]).astype(low)
-    in_copies = sum_begin(17, 0, in_span, every, True)
+    in_copies = sum_next(22, 0, in_span, every, "east", in_copies)
     wait(copies)
     wait_some(pending)
     first = half * head_dim
@@ -1110,8 +1143,8 @@
     )
     R.small[0, :] = jnp.sum(grad_conv.astype(f32), axis=0)
     small_copy = send(21, 0, R.small, R.small_got.at[0], twin, "dp")
-    out_copies = sum_next(23, 1, out_span, every, False, out_copies)
-    in_copies = sum_next(22, 0, in_span, every, True, in_copies)
+    out_copies = sum_next(23, 1, out_span, every, "level", out_copies)
+    in_copies = sum_last(38, 0, every, "east", in_copies)
     mixed_pending = move(36, R.mixed_here, R.mixed_got, from_level_device)
     wait_some(conv_pending)
     @pl.loop(0, groups)
@@ -1129,18 +1162,51 @@
     )
     R.back_home[row_block(me, channels), :] = R.result[:, lane_block(me)]
 
+    out_copies = sum_last(37, 1, every, "level", out_copies)
+
     wait(late)
     wait_some(left_pending)
     product = matmul_turned(R.late_left[...], R.late_right[...])
     R.in_w[:, chunk_of(2)] = product.astype(low)
     middle = width // 2
     parts = (
-        (26, slice(2 * width, 2 * width + middle), slice(0, middle), True),
-        (28, slice(2 * width + middle, 3 * width), slice(middle, width), False),
+        (26, slice(2 * width, 2 * width + middle), slice(0, middle), "side"),
+        (28, slice(2 * width + middle, 3 * width), slice(middle, width), "level"),
     )
     att_copies = [sum_begin(kind, 2, source, span, first) for kind, source, span, first in parts]
-    out_copies = sum_last(37, 1, every, False, out_copies)
+    def slots_of(ref):
+        return lambda index: ref.at[index]
+
+    settled = side == east
+    R.in_part[...] = summed(0, in_copies)
+
+    def in_send(step, source, slot, device):
+        return pltpu.make_async_remote_copy(
+            src_ref=source,
+            dst_ref=R.in_sums.at[slot],
+            send_sem=R.out_sem.at[40, step],
+            recv_sem=R.in_sem.at[40, step],
+            device_id=device,
+            device_id_type=MESH,
+        )
+
+    in_near = in_send(0, R.in_part, corner, {"blk": near})
+    in_far = [
+        in_send(1 + n, R.in_sums.at[slot], slot, {"dp": across})
+        for n, slot in enumerate((corner, facing))
+    ]
+
+    @pl.when(jnp.logical_not(settled))
+    def _():
+        in_near.start()
+
+    @pl.when(settled)
+    def _():
+        R.in_sums[corner] = R.in_part[...]
+        in_far[0].start()
+
     quarter = channels // rows_count
+
     @pl.loop(0, groups)
     def _(group):
         grad = matmul_turned(R.shifted[group], R.taps[group])
@@ -1156,35 +1222,32 @@
     small_copy.wait()
     R.small_sum[0] = R.small[...] + R.small_got[0]
     small_copy = send(21, 1, R.small_sum.at[0], R.small_got.at[1], across, "dp")
-    in_copies = sum_last(38, 0, every, True, in_copies)
-    att_copies = [
-        sum_next(kind + 1, 2, source, span, first, copies)
-        for (kind, source, span, first), copies in zip(parts, att_copies)
-    ]
     conv_copy.wait()
     for part in range(2):
         R.conv_sum[part] = (
             R.conv_part[part, core].astype(f32) + R.conv_got[part].astype(f32)
         ).astype(low)
     conv_copy = send(25, 1, R.conv_sum.at[1 - row // 2], R.conv_far, across, "dp")
+    R.out_sums[row] = summed(1, out_copies)
+    out_share = share_start(43, slots_of(R.out_sums))
+    att_copies = [
+        sum_next(kind + 1, 2, source, span, first, copies)
+        for (kind, source, span, first), copies in zip(parts, att_copies)
+    ]
+    @pl.when(settled)
+    def _():
+        in_near.wait_recv()
+        in_far[1].start()
+
     small_copy.wait()
     R.small_sum[1] = R.small_sum[0] + R.small_got[1]
     small_copy = send(21, 2, R.small_sum.at[1], R.small_got.at[2], near)
 
-    def slots_of(ref):
-        return lambda index: ref.at[index]
-
-    def part_of(ref, which):
-        return lambda index: ref.at[index, which]
-
-    R.ffn_sums[row, 1] = summed(1, out_copies)
-    out_share = share_start(43, part_of(R.ffn_sums, 1))
-    R.ffn_sums[row, 0] = summed(0, in_copies)
-    in_share = share_start(40, part_of(R.ffn_sums, 0))
     att_copies = [
         sum_last(kind + 13, 2, span, first, copies)
         for (kind, source, span, first), copies in zip(parts, att_copies)
     ]
+    share_forward(43, slots_of(R.out_sums), out_share)
     wait(back)
     wait_some(mixed_pending)
     R.frames_done[...] = (
@@ -1206,17 +1269,33 @@
         smalls.append(
             send(30, step, R.small_far.at[level], R.small_far.at[level], target)
         )
-    share_forward(43, part_of(R.ffn_sums, 1), out_share)
-    share_forward(40, part_of(R.ffn_sums, 0), in_share)
+
     R.attn_sums[row] = summed(2, att_copies[0] + att_copies[1])
     att_share = share_start(31, slots_of(R.attn_sums))
     share_forward(42, slots_of(R.conv_sums), conv_share)
     wait(smalls)
     R.small_done[...] = sum_parts(R.small_far)
     store(2, R.small_done, R.small_out)
+
+    @pl.when(settled)
+    def _():
+        in_far[0].wait_send()
+        in_far[1].wait_send()
+
+    @pl.when(jnp.logical_not(settled))
+    def _():
+        in_near.wait_send()
+        in_far[0].wait_recv()
+        in_far[1].wait_recv()
+
+    in_share = [
+        send(40, 3 + n, R.in_sums.at[slot], R.in_sums.at[slot], twin, "dp")
+        for n, slot in enumerate((corner, facing))
+    ]
     wait(out_share)
+    store(3, R.out_sums, R.back_out)
     wait(in_share)
-    store(3, R.ffn_sums, R.ffn_out)
+    store(6, R.in_sums, R.in_out)
     wait(conv_share)
     store(4, R.conv_sums, R.conv_out)
     share_forward(31, slots_of(R.attn_sums), att_share)
@@ -1258,7 +1337,8 @@
         "layer_out": ((tokens, width), low),
         "frames_out": ((tokens, width), low),
         "conv_out": ((rows_count, piece, group_width, kernel), low),
-        "ffn_out": ((rows_count, 2, channels, width), low),
+        "in_out": ((rows_count, channels, width), low),
+        "back_out": ((rows_count, channels, width), low),
         "attn_out": ((rows_count, channels, width), low),
         "small_out": ((16, width), f32),
     }
@@ -1331,7 +1411,9 @@
         "layer_got": ((tokens, width), low),
         "frames_done": ((tokens, width), low),
         "small_done": ((16, width), f32),
-        "ffn_sums": ((rows_count, 2, channels, width), low),
+        "in_sums": ((rows_count, channels, width), low),
+        "in_part": ((channels, width), low),
+        "out_sums": ((rows_count, channels, width), low),
         "conv_sums": ((rows_count, piece, group_width, kernel), low),
         "attn_sums": ((rows_count, channels, width), low),
         "conv_part": ((2, 2, piece, group_width, kernel), low),
@@ -1348,8 +1430,8 @@
         out_specs=(hbm,) * len(outs),
         scratch_shapes=[pltpu.VMEM(*item) for item in scratch.values()]
         + [
-            pltpu.SemaphoreType.DMA((44, count)),
-            pltpu.SemaphoreType.DMA((44, count)),
+            pltpu.SemaphoreType.DMA((45, count)),
+            pltpu.SemaphoreType.DMA((45, count)),
             pltpu.SemaphoreType.DMA((3 + 2 * (wide // width),)),
             pltpu.SemaphoreType.DMA((len(outs),)),
         ],
@@ -1365,7 +1447,8 @@
     layer_hbm,
     frames_hbm,
     conv_hbm,
-    ffn_hbm,
+    in_hbm,
+    back_hbm,
     attn_hbm,
     small_hbm,
     layer_out,
@@ -1390,7 +1473,8 @@
     in_wide,
     back_wide,
     conv_ref,
-    ffn_ref,
+    in_ref,
+    back_ref,
     attn_ref,
     small_ref,
     layer_ref,
@@ -1414,7 +1498,8 @@
         for i, (source, target) in enumerate(
             (
                 (conv_hbm, conv_ref),
-                (ffn_hbm, ffn_ref),
+                (in_hbm, in_ref),
+                (back_hbm, back_ref),
                 (attn_hbm, attn_ref),
                 (small_hbm, small_ref),
                 (layer_hbm, layer_ref),
@@ -1430,25 +1515,24 @@
         conv_wide[part] = conv_ref[row].astype(f32)
         start(conv_wide.at[part], conv_out.at[part])
     loads[1].wait()
+    for row in range(rows_count):
+        in_wide[:, row * width : (row + 1) * width] = in_ref[row].astype(f32)
+    start(in_wide, in_out)
     loads[2].wait()
     for row in range(rows_count):
-        part = slice(row * channels, (row + 1) * channels)
-        span = slice(row * width, (row + 1) * width)
-        in_wide[:, span] = ffn_ref[row, 0].astype(f32)
-        back_wide[part, :] = ffn_ref[row, 1].astype(f32)
-        if row < rows_count - 1:
-            qkv_wide[:, span] = attn_ref[row].astype(f32)
-        else:
-            out_wide[...] = attn_ref[row].astype(f32)
-    start(in_wide, in_out)
+        back_wide[row * channels : (row + 1) * channels, :] = back_ref[row].astype(f32)
     start(back_wide, back_out)
+    loads[3].wait()
+    for row in range(rows_count - 1):
+        qkv_wide[:, row * width : (row + 1) * width] = attn_ref[row].astype(f32)
     start(qkv_wide, qkv_out)
+    out_wide[...] = attn_ref[rows_count - 1].astype(f32)
     start(out_wide, out_out)
+    loads[5].wait()
+    start(layer_ref, layer_out)
+    loads[6].wait()
+    start(frames_ref, frames_out)
     loads[4].wait()
-    start(layer_ref, layer_out)
-    loads[5].wait()
-    start(frames_ref, frames_out)
-    loads[3].wait()
     small = small_ref[...]
     own = pltpu.roll(small, lax.rem(width - channels * me, width), 1)
     for place, ref in (
@@ -1470,7 +1554,7 @@
         copy.wait()
 
 
-def unpack(count, layer_out, frames_out, conv, ffn, attn, small):
+def unpack(count, layer_out, frames_out, conv, ffn_in, ffn_out, attn, small):
     rows_count, channels, width = attn.shape
     piece, group_width, kernel = conv.shape[1:]
     f32 = jnp.float32
@@ -1501,7 +1585,7 @@
             vector,
             vector,
         ),
-        in_specs=[hbm] * 6,
+        in_specs=[hbm] * 7,
         out_specs=(
             hbm,
             hbm,
@@ -1524,11 +1608,11 @@
             pltpu.VMEM(item.shape, f32)
             for item in (conv_type, qkv_type, out_type, in_type, back_type)
         ]
-        + [pltpu.VMEM(item.shape, item.dtype) for item in (conv, ffn, attn, small, layer_out, frames_out)]
-        + [pltpu.VMEM(small.shape, f32), pltpu.SemaphoreType.DMA((12 + rows_count,))],
+        + [pltpu.VMEM(item.shape, item.dtype) for item in (conv, ffn_in, ffn_out, attn, small, layer_out, frames_out)]
+        + [pltpu.VMEM(small.shape, f32), pltpu.SemaphoreType.DMA((13 + rows_count,))],
         compiler_params=pltpu.CompilerParams(vmem_limit_bytes=62 * 2**20),
         name="unpack",
-    )(layer_out, frames_out, conv, ffn, attn, small)
+    )(layer_out, frames_out, conv, ffn_in, ffn_out, attn, small)
     return (results[0][None], results[1][None], *results[2:])
 
 

time: 165 us -> 157 us (0.952)
  Pallas kernels: 164 us -> 156 us
    pallas_call x1, Pallas kernels: 159 us -> 151 us  [layer(): pl.pallas_call(functools.partial(layer_kernel, names, count, rows_count,...]
where the time goes in v1:
time: 157 us
  Pallas kernels  156 us (99%)
    pallas_call x1, Pallas kernels, layer(): pl.pallas_call(functools.partial(layer_kernel, names, count, rows_count,...  151 us
    pallas_call x1, Pallas kernels, unpack(): pl.pallas_call(functools.partial(unpack_kernel, count), out_shape=(jax.Sh...  4.69 us

profile of v1, /device:TPU:0, one launch (start us, length us, event | category | flops | bytes accessed | tf_op | source)
XLA Modules:
  0.0 156.6 jit_solution(4380112771641879345)
XLA Ops:
  0.7 151.1 %layer.1 = (bf16[128,768]{1,0:T(8,128)(2,1)}, bf16[128,768]{1,0:T(8,128)(2,1)}, bf16[4,24,48,128]{3,2,1,0:T(8,128)(2,1)}, bf16[4,96,768]{2,1,0:T(8,128)(2,1)}, b...) custom-call(bf16[128,768]{1,0:T(8,128)(2,1)} %bitcast.4, s32[1,128]{1,0:T(1,128)} %refs_1_.1, ...), custom_call_target="tpu_custom_call" | custom-call | tf_op jit(solution)/shard_map/layer/pallas_call | solution.py:1426
  151.8 4.7 %unpack.1 = (bf16[128,768]{1,0:T(8,128)(2,1)}, bf16[128,768]{1,0:T(8,128)(2,1)}, f32[96,48,128]{2,1,0:T(8,128)}, f32[96]{0:T(128)}, f32[96,2304]{1,0:T(8,128)}, ...) custom-call(bf16[128,768]{1,0:T(8,128)(2,1)} %get-tuple-element.39.l, ...), custom_call_target="tpu_custom_call" | custom-call | tf_op jit(solution)/shard_map/unpack/pallas_call | solution.py:1568

commit v2 on v1

--- a/solution.py
+++ b/solution.py
@@ -535,7 +535,7 @@
     corner = 2 * side + core
     facing = peer(corner, 2, 4)
     across = peer(row, 2, rows_count)
-    tokens, width = R.frames.shape
+    tokens, width = R.frames_hbm.shape
     channels = width // count
     length = count * LANES
     group_width = R.own_weight.shape[1]
@@ -656,6 +656,15 @@
         R.conv_hbm.at[row_block(me, channels)], R.own_weight, R.load_sem.at[2 + 2 * chunks]
     )
     own_load.start()
+    first_loads = [
+        pltpu.make_async_copy(source, target, R.first_sem.at[index])
+        for index, (source, target) in enumerate(
+            ((R.frames_hbm, R.frames), (R.cotangent_hbm, R.cotangent))
+        )
+    ]
+    for load in first_loads:
+        load.start()
+    first_loads[0].wait()
     valid = (R.segment[...] >= 0).astype(f32)
     R.turned[...] = (R.frames[...].astype(f32).T * valid).astype(low)
     to_level_device = device_at(me, core)
@@ -691,14 +700,14 @@
     copies = to_blocks(
         0, lambda p: R.turned.at[row_block(p, channels), :], R.column.at[:, lane_block(me + 1)]
     )
-    brought = move(33, R.frames, R.frames_home, to_level_device)
-    seg_pending = to_level(1, lambda p: R.segment, R.segs.at[me])
     R.column[:, lane_block(me + 1)] = R.turned[row_block(me, channels), :]
     for ref in (R.column, R.gcol):
         ref[:, :LANES] = jnp.zeros((channels, LANES), low)
         ref[:, length + LANES :] = jnp.zeros((channels, LANES), low)
     mix_taps(R.mix_back, lambda g, c: pl.ds(g * square + c * group_width, group_width))
     wait(copies)
+    brought = move(33, R.frames, R.frames_home, to_level_device)
+    seg_pending = to_level(1, lambda p: R.segment, R.segs.at[me])
 
     @pl.loop(0, groups)
     def _(group):
@@ -727,7 +736,6 @@
     clip_column(count, R.segs, R.clip)
     wait_some(brought)
     wait_some(pending)
-    brought = move(34, R.cotangent, R.cotangent_home, to_level_device)
 
     pre = R.conv_home[...].astype(f32).T + table(0)
     share = 0.5 * (1.0 + lax.erf(pre * ROOT_HALF))
@@ -838,6 +846,8 @@
         R.att_home[extra_rows, :] = R.low_extra[:, lane_block(pos)]
 
     wait(copies)
+    first_loads[1].wait()
+    brought = move(34, R.cotangent, R.cotangent_home, to_level_device)
 
     @pl.loop(0, length // size)
     def _(block):
@@ -898,7 +908,6 @@
     R.act_all[:, :, lane_block(row)] = R.act_turned[:, row]
     layer, normed_two, inv_two = norm_forward(R.total[...], table(11), table(12))
     R.layer_here[...] = layer.astype(low)
-    layer_pending = move(35, R.layer_here, R.layer_got, from_level_device)
     wait_some(brought)
     grad_second, gain_sum, shift_sum = norm_backward(
         R.cotangent_home[...].astype(f32), normed_two, inv_two, table(11)
@@ -948,6 +957,8 @@
     R.pre_all[:, lane_block(corner)] = R.pre_turned[corner]
     R.dproject[3] = turned(grad_branch)
     wait(extra_copies)
+    layer_pending = move(35, R.layer_here, R.layer_got, from_level_device)
+    share_forward(10, lanes_of(R.two_all), two_copies)
 
     def attend_back(held, grads, start, index, att, lse):
         queries = held[0, :, start]
@@ -1072,8 +1083,6 @@
         copy.start()
         stores.append(copy)
 
-    share_forward(10, lanes_of(R.two_all), two_copies)
-    share_forward(7, lanes_of(R.hidden_all), hidden_copies, facing)
     blocks = length // size
 
     def main_back(block):
@@ -1101,12 +1110,13 @@
 
     R.dkey[...] = jnp.zeros_like(R.dkey)
     R.dvalue[...] = jnp.zeros_like(R.dvalue)
-    pl.loop(0, blocks // 2)(main_back)
+    share_forward(7, lanes_of(R.hidden_all), hidden_copies, facing)
     wait(two_copies)
     wait(act_copies)
     product = matmul_turned(R.act_all[...].reshape(width, -1), R.two_all[...])
     R.in_w[:, out_span] = product.astype(low)
     out_copies = sum_begin(18, 1, out_span, every, "level")
+    pl.loop(0, blocks // 2)(main_back)
     wait(hidden_copies)
     wait(pre_copies)
     R.in_w[:, in_span] = matmul_turned(R.hidden_all[...], R.pre_all[...]).astype(low)
@@ -1119,7 +1129,7 @@
     )
     copies += [query_copy(peer(pos, step, count)) for step in range(1, count)]
     R.dproject[0:3, own_rows, :] = R.dmain[:, :, lane_block(pos)]
-    in_copies = sum_next(22, 0, in_span, every, "east", in_copies)
+    out_copies = sum_next(23, 1, out_span, every, "level", out_copies)
     wait(copies)
     wait_some(pending)
     first = half * head_dim
@@ -1143,27 +1153,8 @@
     )
     R.small[0, :] = jnp.sum(grad_conv.astype(f32), axis=0)
     small_copy = send(21, 0, R.small, R.small_got.at[0], twin, "dp")
-    out_copies = sum_next(23, 1, out_span, every, "level", out_copies)
-    in_copies = sum_last(38, 0, every, "east", in_copies)
-    mixed_pending = move(36, R.mixed_here, R.mixed_got, from_level_device)
-    wait_some(conv_pending)
-    @pl.loop(0, groups)
-    def _(group):
-        rows = row_block(group, group_width)
-        spread_taps(R.gcol[rows, :].astype(f32), LANES // 2, -1, R.stage, R.taps.at[group])
-        product = dot(R.mix_back[group], R.taps[group])
-        total = product[:group_width, LANES:]
-        for a in range(1, steps):
-            part = product[a * group_width : (a + 1) * group_width, :]
-            total = total + pltpu.roll(part, a * TAP_STEP, 1)[:, LANES:]
-        R.result[rows, :] = total.astype(low)
-    back = to_blocks(
-        24, lambda p: R.result.at[:, lane_block(p)], R.back_home.at[row_block(me, channels), :]
-    )
-    R.back_home[row_block(me, channels), :] = R.result[:, lane_block(me)]
-
+    in_copies = sum_next(22, 0, in_span, every, "east", in_copies)
     out_copies = sum_last(37, 1, every, "level", out_copies)
-
     wait(late)
     wait_some(left_pending)
     product = matmul_turned(R.late_left[...], R.late_right[...])
@@ -1174,36 +1165,13 @@
         (28, slice(2 * width + middle, 3 * width), slice(middle, width), "level"),
     )
     att_copies = [sum_begin(kind, 2, source, span, first) for kind, source, span, first in parts]
-    def slots_of(ref):
-        return lambda index: ref.at[index]
-
-    settled = side == east
-    R.in_part[...] = summed(0, in_copies)
-
-    def in_send(step, source, slot, device):
-        return pltpu.make_async_remote_copy(
-            src_ref=source,
-            dst_ref=R.in_sums.at[slot],
-            send_sem=R.out_sem.at[40, step],
-            recv_sem=R.in_sem.at[40, step],
-            device_id=device,
-            device_id_type=MESH,
-        )
-
-    in_near = in_send(0, R.in_part, corner, {"blk": near})
-    in_far = [
-        in_send(1 + n, R.in_sums.at[slot], slot, {"dp": across})
-        for n, slot in enumerate((corner, facing))
-    ]
-
-    @pl.when(jnp.logical_not(settled))
-    def _():
-        in_near.start()
-
-    @pl.when(settled)
-    def _():
-        R.in_sums[corner] = R.in_part[...]
-        in_far[0].start()
+    wait_some(conv_pending)
+    mixed_pending = move(36, R.mixed_here, R.mixed_got, from_level_device)
+
+    @pl.loop(0, groups)
+    def _(group):
+        rows = row_block(group, group_width)
+        spread_taps(R.gcol[rows, :].astype(f32), LANES // 2, -1, R.stage, R.taps.at[group])
 
     quarter = channels // rows_count
 
@@ -1219,25 +1187,65 @@
                 channel = block * steps + u
                 R.conv_part[group, channel // quarter, channel % quarter] = tile.astype(low)
     conv_copy = send(25, 0, R.conv_part.at[:, 1 - core], R.conv_got, twin, "dp")
-    small_copy.wait()
-    R.small_sum[0] = R.small[...] + R.small_got[0]
-    small_copy = send(21, 1, R.small_sum.at[0], R.small_got.at[1], across, "dp")
+    in_copies = sum_last(38, 0, every, "east", in_copies)
+    def slots_of(ref):
+        return lambda index: ref.at[index]
+
+    R.out_sums[row] = summed(1, out_copies)
+    out_share = share_start(43, slots_of(R.out_sums))
+    @pl.loop(0, groups)
+    def _(group):
+        rows = row_block(group, group_width)
+        product = dot(R.mix_back[group], R.taps[group])
+        total = product[:group_width, LANES:]
+        for a in range(1, steps):
+            part = product[a * group_width : (a + 1) * group_width, :]
+            total = total + pltpu.roll(part, a * TAP_STEP, 1)[:, LANES:]
+        R.result[rows, :] = total.astype(low)
+    back = to_blocks(
+        24, lambda p: R.result.at[:, lane_block(p)], R.back_home.at[row_block(me, channels), :]
+    )
+    R.back_home[row_block(me, channels), :] = R.result[:, lane_block(me)]
     conv_copy.wait()
     for part in range(2):
         R.conv_sum[part] = (
             R.conv_part[part, core].astype(f32) + R.conv_got[part].astype(f32)
         ).astype(low)
     conv_copy = send(25, 1, R.conv_sum.at[1 - row // 2], R.conv_far, across, "dp")
-    R.out_sums[row] = summed(1, out_copies)
-    out_share = share_start(43, slots_of(R.out_sums))
     att_copies = [
         sum_next(kind + 1, 2, source, span, first, copies)
         for (kind, source, span, first), copies in zip(parts, att_copies)
     ]
+    small_copy.wait()
+    R.small_sum[0] = R.small[...] + R.small_got[0]
+    small_copy = send(21, 1, R.small_sum.at[0], R.small_got.at[1], across, "dp")
+    settled = side == east
+    R.in_part[...] = summed(0, in_copies)
+
+    def in_send(step, source, slot, device):
+        return pltpu.make_async_remote_copy(
+            src_ref=source,
+            dst_ref=R.in_sums.at[slot],
+            send_sem=R.out_sem.at[40, step],
+            recv_sem=R.in_sem.at[40, step],
+            device_id=device,
+            device_id_type=MESH,
+        )
+
+    in_near = in_send(0, R.in_part, corner, {"blk": near})
+    in_far = [
+        in_send(1 + n, R.in_sums.at[slot], slot, {"dp": across})
+        for n, slot in enumerate((corner, facing))
+    ]
+
+    @pl.when(jnp.logical_not(settled))
+    def _():
+        in_near.start()
+
     @pl.when(settled)
     def _():
-        in_near.wait_recv()
-        in_far[1].start()
+        R.in_sums[corner] = R.in_part[...]
+        in_far[0].start()
 
     small_copy.wait()
     R.small_sum[1] = R.small_sum[0] + R.small_got[1]
@@ -1261,6 +1269,11 @@
         R.conv_sum[row // 2].astype(f32) + R.conv_far[...].astype(f32)
     ).astype(low)
     conv_share = share_start(42, slots_of(R.conv_sums))
+    @pl.when(settled)
+    def _():
+        in_near.wait_recv()
+        in_far[1].start()
+
     small_copy.wait()
     R.small_far[level] = R.small_sum[1] + R.small_got[2]
     smalls = []
@@ -1320,7 +1333,7 @@
 
 def layer(count, rows_count, head_dim, named):
     low, f32 = jnp.bfloat16, jnp.float32
-    tokens, width = named["frames"].shape
+    tokens, width = named["frames_hbm"].shape
     wide = named["in_hbm"].shape[1]
     _, group_width, kernel = named["conv_hbm"].shape
     channels = width // count
@@ -1361,6 +1374,8 @@
         "stage": ((span // LANES * taps, LANES), f32),
         "own_weight": ((channels, group_width, kernel), low),
         "frames_home": ((tokens, width), low),
+        "frames": ((tokens, width), low),
+        "cotangent": ((tokens, width), low),
         "cotangent_home": ((tokens, width), low),
         "layer_here": ((tokens, width), low),
         "mixed_here": ((tokens, width), low),
@@ -1422,7 +1437,7 @@
         "conv_far": ((piece, group_width, kernel), low),
     }
     hbm = pl.BlockSpec(memory_space=pl.ANY)
-    names = (*named, *outs, *scratch, "out_sem", "in_sem", "load_sem", "store_sem")
+    names = (*named, *outs, *scratch, "out_sem", "in_sem", "load_sem", "store_sem", "first_sem")
     return pl.pallas_call(
         functools.partial(layer_kernel, names, count, rows_count, head_dim),
         out_shape=tuple(jax.ShapeDtypeStruct(*out) for out in outs.values()),
@@ -1434,6 +1449,7 @@
             pltpu.SemaphoreType.DMA((45, count)),
             pltpu.SemaphoreType.DMA((3 + 2 * (wide // width),)),
             pltpu.SemaphoreType.DMA((len(outs),)),
+            pltpu.SemaphoreType.DMA((2,)),
         ],
         compiler_params=pltpu.CompilerParams(
             collective_id=0, has_side_effects=True, vmem_limit_bytes=62 * 2**20
@@ -1663,9 +1679,9 @@
     cotangent,
 ):
     named = {
-        "frames": frames[0],
+        "frames_hbm": frames[0],
         "segment": segment,
-        "cotangent": cotangent[0],
+        "cotangent_hbm": cotangent[0],
         "conv_bias": conv_bias,
         "qv_bias": qv_bias,
         "out_bias": out_bias,

time: 157 us -> 152 us (0.968)
  Pallas kernels: 156 us -> 150 us
    pallas_call x1, Pallas kernels: 151 us -> 145 us  [layer(): pl.pallas_call(functools.partial(layer_kernel, names, count, rows_count,...]
where the time goes in v2:
time: 152 us; the launch traced here: 151 us
  Pallas kernels  150 us (99%)
    pallas_call x1, Pallas kernels, layer(): pl.pallas_call(functools.partial(layer_kernel, names, count, rows_count,...  145 us
    pallas_call x1, Pallas kernels, unpack(): pl.pallas_call(functools.partial(unpack_kernel, count), out_shape=(jax.Sh...  4.69 us

profile of v2, /device:TPU:0, one launch (start us, length us, event | category | flops | bytes accessed | tf_op | source)
XLA Modules:
  0.0 150.8 jit_solution(15982854750933706111)
XLA Ops:
  0.7 145.3 %layer.1 = (bf16[128,768]{1,0:T(8,128)(2,1)}, bf16[128,768]{1,0:T(8,128)(2,1)}, bf16[4,24,48,128]{3,2,1,0:T(8,128)(2,1)}, bf16[4,96,768]{2,1,0:T(8,128)(2,1)}, b...) custom-call(bf16[128,768]{1,0:T(8,128)(2,1)} %bitcast.4, s32[1,128]{1,0:T(1,128)} %refs_1_.1, ...), custom_call_target="tpu_custom_call" | custom-call | tf_op jit(solution)/shard_map/layer/pallas_call | solution.py:1441
  146.0 4.7 %unpack.1 = (bf16[128,768]{1,0:T(8,128)(2,1)}, bf16[128,768]{1,0:T(8,128)(2,1)}, f32[96,48,128]{2,1,0:T(8,128)}, f32[96]{0:T(128)}, f32[96,2304]{1,0:T(8,128)}, ...) custom-call(bf16[128,768]{1,0:T(8,128)(2,1)} %get-tuple-element.39.l, ...), custom_call_target="tpu_custom_call" | custom-call | tf_op jit(solution)/shard_map/unpack/pallas_call | solution.py:1584

commit v3 on v2

--- a/solution.py
+++ b/solution.py
@@ -1155,16 +1155,6 @@
     small_copy = send(21, 0, R.small, R.small_got.at[0], twin, "dp")
     in_copies = sum_next(22, 0, in_span, every, "east", in_copies)
     out_copies = sum_last(37, 1, every, "level", out_copies)
-    wait(late)
-    wait_some(left_pending)
-    product = matmul_turned(R.late_left[...], R.late_right[...])
-    R.in_w[:, chunk_of(2)] = product.astype(low)
-    middle = width // 2
-    parts = (
-        (26, slice(2 * width, 2 * width + middle), slice(0, middle), "side"),
-        (28, slice(2 * width + middle, 3 * width), slice(middle, width), "level"),
-    )
-    att_copies = [sum_begin(kind, 2, source, span, first) for kind, source, span, first in parts]
     wait_some(conv_pending)
     mixed_pending = move(36, R.mixed_here, R.mixed_got, from_level_device)
 
@@ -1187,6 +1177,16 @@
                 channel = block * steps + u
                 R.conv_part[group, channel // quarter, channel % quarter] = tile.astype(low)
     conv_copy = send(25, 0, R.conv_part.at[:, 1 - core], R.conv_got, twin, "dp")
+    wait(late)
+    wait_some(left_pending)
+    product = matmul_turned(R.late_left[...], R.late_right[...])
+    R.in_w[:, chunk_of(2)] = product.astype(low)
+    middle = width // 2
+    parts = (
+        (26, slice(2 * width, 2 * width + middle), slice(0, middle), "side"),
+        (28, slice(2 * width + middle, 3 * width), slice(middle, width), "level"),
+    )
+    att_copies = [sum_begin(kind, 2, source, span, first) for kind, source, span, first in parts]
     in_copies = sum_last(38, 0, every, "east", in_copies)
     def slots_of(ref):
         return lambda index: ref.at[index]
@@ -1251,6 +1251,11 @@
     R.small_sum[1] = R.small_sum[0] + R.small_got[1]
     small_copy = send(21, 2, R.small_sum.at[1], R.small_got.at[2], near)
 
+    conv_copy.wait()
+    R.conv_sums[row] = (
+        R.conv_sum[row // 2].astype(f32) + R.conv_far[...].astype(f32)
+    ).astype(low)
+    conv_share = share_start(42, slots_of(R.conv_sums))
     att_copies = [
         sum_last(kind + 13, 2, span, first, copies)
         for (kind, source, span, first), copies in zip(parts, att_copies)
@@ -1264,11 +1269,6 @@
     store(0, R.frames_done, R.frames_out)
     wait_some(layer_pending)
     store(1, R.layer_got, R.layer_out)
-    conv_copy.wait()
-    R.conv_sums[row] = (
-        R.conv_sum[row // 2].astype(f32) + R.conv_far[...].astype(f32)
-    ).astype(low)
-    conv_share = share_start(42, slots_of(R.conv_sums))
     @pl.when(settled)
     def _():
         in_near.wait_recv()
@@ -1283,9 +1283,9 @@
             send(30, step, R.small_far.at[level], R.small_far.at[level], target)
         )
 
+    share_forward(42, slots_of(R.conv_sums), conv_share)
     R.attn_sums[row] = summed(2, att_copies[0] + att_copies[1])
     att_share = share_start(31, slots_of(R.attn_sums))
-    share_forward(42, slots_of(R.conv_sums), conv_share)
     wait(smalls)
     R.small_done[...] = sum_parts(R.small_far)
     store(2, R.small_done, R.small_out)

time: 152 us -> 152 us (level)
  no operation moved by 1% of the time
where the time goes in v3:
time: 152 us; the launch traced here: 150 us
  Pallas kernels  150 us (99%)
    pallas_call x1, Pallas kernels, layer(): pl.pallas_call(functools.partial(layer_kernel, names, count, rows_count,...  145 us
    pallas_call x1, Pallas kernels, unpack(): pl.pallas_call(functools.partial(unpack_kernel, count), out_shape=(jax.Sh...  4.69 us

profile of v3, /device:TPU:0, one launch (start us, length us, event | category | flops | bytes accessed | tf_op | source)
XLA Modules:
  0.0 150.4 jit_solution(9416468574769979420)
XLA Ops:
  0.7 144.9 %layer.1 = (bf16[128,768]{1,0:T(8,128)(2,1)}, bf16[128,768]{1,0:T(8,128)(2,1)}, bf16[4,24,48,128]{3,2,1,0:T(8,128)(2,1)}, bf16[4,96,768]{2,1,0:T(8,128)(2,1)}, b...) custom-call(bf16[128,768]{1,0:T(8,128)(2,1)} %bitcast.4, s32[1,128]{1,0:T(1,128)} %refs_1_.1, ...), custom_call_target="tpu_custom_call" | custom-call | tf_op jit(solution)/shard_map/layer/pallas_call | solution.py:1441
  145.5 4.7 %unpack.1 = (bf16[128,768]{1,0:T(8,128)(2,1)}, bf16[128,768]{1,0:T(8,128)(2,1)}, f32[96,48,128]{2,1,0:T(8,128)}, f32[96]{0:T(128)}, f32[96,2304]{1,0:T(8,128)}, ...) custom-call(bf16[128,768]{1,0:T(8,128)(2,1)} %get-tuple-element.39.l, ...), custom_call_target="tpu_custom_call" | custom-call | tf_op jit(solution)/shard_map/unpack/pallas_call | solution.py:1584
